TPU v7x, 32 devices: a whole 2x2x4 slice. The times are simulated.
32 devices in a mesh: patch: 8 (over z, y), trial: 4 (over x, core).
Axes of the slice: x: 2, y: 2, z: 4, core: 2. Of those that a mesh axis runs over, the one named last changes fastest.
Arguments:
- activity: float32 [32, 32768], P('trial', 'patch'), may hold values from 0 to 1
- history: bfloat16 [7, 32, 32768], P(None, 'trial', 'patch'), may hold values from 0 to 1
- drive: float32 [32768], P('patch'), may hold values from -6 to 6
- slope: float32 [32], P('trial'), may hold values from 0.5 to 2
- strength: float32 [32], P('trial'), may hold values from 0.1 to 1
- kernel: bfloat16 [256, 4, 128, 128], P('patch', 'trial'), may hold values from -0.25 to 0.25
- kernel_index: int32 [256, 4], P('patch'), may hold values from 0 to 33, as said below
- tract_source: int32 [1024], P('patch'), may hold values from 0 to 31
- tract_delay: int32 [1024], P('patch'), may hold values from 4 to 7
- tract_target: int32 [1024, 1], P('patch'), may hold values from 0 to 7; in each aligned block of 128 rows (0 to 127, 128 to 255, ...) at most 17 rows name the same one
- tract_block: int32 [1024], P('patch'), may hold values from 0 to 31
- tract_weight: float32 [1024], P('patch'), may hold values from 0.25 to 2
- voxel_owner: int32 [32768], P('patch'), may hold values from 0 to 991, as said below
- vaso_signal: float32 [32, 1024], P('trial', 'patch'), may hold values from -3 to 3
- blood_flow: float32 [32, 1024], P('trial', 'patch'), may hold values from 0.5 to 1.5
Outputs:
- activity_out: float32 [32, 32768], P('trial', 'patch')
- vaso_out: float32 [32, 1024], P('trial', 'patch')
- flow_out: float32 [32, 1024], P('trial', 'patch')
Inputs may be any that keep to these rules, and one draw needn't show every extreme that they name: `kernel_index`: block b of a patch lists itself (entry b + 1) first; its other entries name b, b + 1 or b + 2; block 0's second entry is 0 and the last block's third entry is 33. `tract_target`: among the 128 tracts of one patch no target patch is named more than 17 times. `voxel_owner`: A vertex of patch p lies in a voxel owned by patch p - 1, p or p + 1, where patch p owns voxels p * 128 to (p + 1) * 128 - 1; the last quarter of each patch's voxels hold no vertex.
All inputs are finite; a program needn't handle non-finite values.
Results may differ from a plain program's by a relative error of at most 0.00037.
Values may be sent and summed in bfloat16 or wider, within the bound.
A program may use at most 64 MiB of HBM per device.

v0:
```python
import jax
import jax.numpy as jnp
from jax import lax
from jax.sharding import PartitionSpec as P

BLOCK = 128
STEPS = 4
HIST = 7


def extended_2(array, sides, width):
    for axis, dim in sides:
        peers, length = (lax.axis_size(axis), array.shape[dim])
        up = [(i, (i + 1) % peers) for i in range(peers - 1)]
        down = [(j, i) for i, j in up]
        last = lax.slice_in_dim(array, length - width, length, axis=dim)
        leading = lax.slice_in_dim(array, 0, width, axis=dim)
        before = lax.ppermute(last, axis, up)
        after = lax.ppermute(leading, axis, down)
        array = jnp.concatenate([before, array, after], axis=dim)
    return array


def shards(
    activity,
    history,
    drive,
    slope,
    strength,
    kernel,
    kernel_index,
    tract_source,
    tract_delay,
    tract_target,
    tract_block,
    tract_weight,
    voxel_owner,
    vaso_signal,
    blood_flow,
):
    trials_here = activity.shape[0]
    verts = activity.shape[1]
    nblk = verts // BLOCK
    patches = lax.axis_size("patch")
    tracts_here = tract_source.shape[0]
    capacity = max(2, tracts_here // patches + 1)
    slots = patches * capacity
    voxels_here = vaso_signal.shape[1]
    hist_blocks = history.reshape(HIST, trials_here, nblk, BLOCK)
    lag = tract_delay[:, None] - jnp.arange(STEPS, dtype=jnp.int32)[None, :] - 1
    rows = hist_blocks[lag, :, tract_source[:, None], :]
    weighted = (rows.astype(jnp.float32) * tract_weight[:, None, None, None]).astype(jnp.bfloat16)
    target = tract_target[:, 0]
    order = jnp.arange(tracts_here, dtype=jnp.int32)
    same = (target[:, None] == target[None, :]) & (order[None, :] < order[:, None])
    rank = jnp.sum(same.astype(jnp.int32), axis=1)
    slot = target * capacity + rank
    send_rates = jnp.zeros((slots, STEPS, trials_here, BLOCK), jnp.bfloat16).at[slot].set(weighted)
    send_blocks = jnp.full((slots,), -1, jnp.int32).at[slot].set(tract_block)
    got_rates, got_blocks = (
        lax.all_to_all(send_rates, "patch", split_axis=0, concat_axis=0, tiled=True),
        lax.all_to_all(send_blocks, "patch", split_axis=0, concat_axis=0, tiled=True),
    )
    onehot = (got_blocks[None, :] == jnp.arange(nblk, dtype=jnp.int32)[:, None]).astype(
        jnp.bfloat16
    )
    coupling = jnp.einsum("bs,sxtj->xtbj", onehot, got_rates, preferred_element_type=jnp.float32)
    coupling = coupling.reshape(STEPS, trials_here, verts)
    tiles = lax.all_gather(kernel, "trial", axis=1, tiled=True)
    rate = activity
    recorded = []
    for step in range(STEPS):
        rate_b = rate.astype(jnp.bfloat16)
        extended = extended_2(rate_b, (("patch", 1),), BLOCK)
        extended = extended.reshape(trials_here, nblk + 2, BLOCK)
        picked = extended[:, kernel_index]
        local = jnp.einsum("tbki,bkij->tbj", picked, tiles, preferred_element_type=jnp.float32)
        local = local.reshape(trials_here, verts)
        pre = slope[:, None] * (local + strength[:, None] * coupling[step] + drive[None, :])
        rate = rate + 0.5 * (jax.nn.sigmoid(pre) - rate)
        recorded.append(rate)
    values = jnp.concatenate(
        [
            jnp.stack(recorded).reshape(STEPS * trials_here, verts),
            jnp.ones((1, verts), jnp.float32),
        ],
        axis=0,
    )
    offset = (lax.axis_index("patch") - 1) * voxels_here
    partial_value = (
        jnp.zeros((values.shape[0], 3 * voxels_here), jnp.float32)
        .at[:, voxel_owner - offset]
        .add(values)
    )
    widened = extended_2(partial_value, (("patch", 1),), voxels_here)
    mine = (
        widened[:, :voxels_here]
        + widened[:, 2 * voxels_here : 3 * voxels_here]
        + widened[:, 4 * voxels_here :]
    )
    floor = jnp.maximum(mine[-1], 1.0)
    levels = mine[:-1].reshape(STEPS, trials_here, voxels_here) / floor[None, None, :]
    vaso = vaso_signal
    flow = blood_flow
    for step in range(STEPS):
        vaso = vaso + 0.5 * (levels[step] - 0.65 * vaso - 0.41 * (flow - 1.0))
        flow = flow + 0.5 * vaso
    return (rate, vaso, flow)


def solution(mesh):
    placed = (
        P("trial", "patch"),
        P(None, "trial", "patch"),
        P("patch"),
        P("trial"),
        P("trial"),
        P("patch", "trial", None, None),
        P("patch", None),
        P("patch"),
        P("patch"),
        P("patch", None),
        P("patch"),
        P("patch"),
        P("patch"),
        P("trial", "patch"),
        P("trial", "patch"),
    )
    return jax.shard_map(
        shards,
        mesh=mesh,
        in_specs=placed,
        out_specs=(P("trial", "patch"), P("trial", "patch"), P("trial", "patch")),
        check_vma=False,
    )
```

profile of v0, /device:TPU:0, one launch (start us, length us, event | category | flops | bytes accessed | tf_op | source)
XLA Modules:
  0.0 153.2 jit_solution(13333194934178813533)
XLA Ops:
  7.2 0.0 copy-start
  7.2 0.0 all-gather.2.cloned.1.call-start
  7.2 0.7 all-gather.2.cloned.1.call-update
  7.9 0.9 convert_reduce_fusion
  8.8 0.7 fusion.71
  9.5 1.1 scatter_custom_fusion.1
  10.6 0.7 all_to_all.10
  11.3 7.3 %all-to-all-start.1 = ((s32[8,17,1]{1,2,0:T(1,128)}), s32[8,17,1]{1,2,0:T(1,128)S(1)}, u32[]{:S(2)}, u32[]{:S(2)}) async-start(s32[8,17,1]{1,2,0:T(1,128)} %bitcast.12), calls=%async_computation.1 | async-start | bytes 8192 | tf_op jit(solution)/shard_map/all_to_all | solution.py:62
  18.6 0.7 fusion.73
  19.2 0.8 fusion.48
  20.0 0.1 reshape.132
  20.1 2.3 %gather_fusion.1 = bf16[512,8,128]{2,1,0:T(8,128)(2,1)S(1)} fusion(bf16[7,8,32,128]{3,1,2,0:T(8,128)(2,1)S(1)} %bitcast.261, s32[512]{0:T(512)S(1)} %reshape.132), kind=kCustom, calls=%fused_computation.1 | custom fusion | bytes 2101248 | tf_op jit(solution)/shard_map/gather | solution.py:51
  22.4 0.3 fusion.40
  22.7 1.2 broadcast_in_dim.13
  23.9 13.7 %scatter_fusion = bf16[136,4,8,128]{3,2,1,0:T(8,128)(2,1)} fusion(bf16[136,4,8,128]{3,2,1,0:T(8,128)(2,1)} %broadcast_in_dim.13, s32[128]{0:T(128)S(1)} %fusion.71, bf16[128,4,8,128]{3,2,1,0:T(8,128)(2,1)S(1)} %fusion.40), kind=kCustom, calls=%fused_computation.5 | custom fusion | bytes 3146240 | tf_op jit(solution)/shard_map/scatter | solution.py:58
  37.6 0.0 all-to-all-done.1
  37.6 6.0 %all-to-all-start = ((bf16[136,4,8,128]{3,2,1,0:T(8,128)(2,1)}), bf16[136,4,8,128]{3,2,1,0:T(8,128)(2,1)S(1)}, u32[]{:S(2)}, u32[]{:S(2)}) async-start(bf16[136,4,8,128]{3,2,1,0:T(8,128)(2,1)} %scatter_fusion), calls=%async_computation | async-start | bytes 2228224 | tf_op jit(solution)/shard_map/all_to_all | solution.py:61
  43.6 0.0 copy-start.3
  43.6 0.0 copy-start.5
  43.6 0.0 copy-start.6
  43.6 3.9 %collective-permute-start = (bf16[8,128]{1,0:T(8,128)(2,1)S(1)}, bf16[8,128]{1,0:T(8,128)(2,1)S(1)}, u32[]{:S(2)}, u32[]{:S(2)}) collective-permute-start(bf16[8,128]{1,0:T(8,128)(2,1)S(1)} %get-tuple-element.17), channel_id=1, source_target_pairs={{0,4},{4,8},{8,12},{12,16},{16,20},{20,24},{24,28},{1,5},{5,9},{9,... | collective-permute-start | bytes 6152 | tf_op jit(solution)/shard_map/ppermute | solution.py:18
  47.6 1.3 collective-permute-start.1
  48.9 0.1 copy.30
  49.0 0.1 reshape.126
  49.1 0.5 broadcast.212
  49.6 0.7 reduce.5
  50.3 0.1 eq.34
  50.3 0.5 collective-permute-done
  50.8 2.2 %collective-permute-done.1 = bf16[8,128]{1,0:T(8,128)(2,1)S(1)} collective-permute-done((bf16[8,128]{1,0:T(8,128)(2,1)S(1)}, bf16[8,128]{1,0:T(8,128)(2,1)S(1)}, u32[]{:S(2)}, u32[]{:S(2)}) %collective-permute-start.1) | collective-permute-done | bytes 2080 | tf_op jit(solution)/shard_map/ppermute | solution.py:19
  53.1 0.7 gather_fusion
  53.7 16.7 %all-to-all-done = bf16[136,4,8,128]{3,2,1,0:T(8,128)(2,1)S(1)} async-done(((bf16[136,4,8,128]{3,2,1,0:T(8,128)(2,1)}), bf16[136,4,8,128]{3,2,1,0:T(8,128)(2,1)S(1)}, u32[]{:S(2)}, u32[]{:S(2)}) %all-to-all-start) | async-done | bytes 1114144 | tf_op jit(solution)/shard_map/all_to_all | solution.py:61
  70.5 0.5 convolution_bitcast_fusion.4
  71.0 0.0 all-gather.2.cloned.1.call-done
  71.0 2.9 %fusion.82 = (bf16[8,4096]{1,0:T(8,128)(2,1)S(1)}, f32[8,4096]{1,0:T(8,128)S(1)}) fusion(f32[8,4096]{1,0:T(8,128)S(1)} %copy-done.1, f32[4096]{0:T(1024)S(1)} %copy-done.3, f32[1,8,32,128]{3,2,1,0:T(8,128)S(1)} %get-tuple-element.8, f32[8]{0:T(128)S(1)} %copy-done.5, bf16[8,32,4,128]{3,0,2,1:T(8,128)(2,1)S(1)} %bitcast.266, ...), kind=kOutput, calls=%fused_computation.128 | convolution fusion | flops 33914880 | bytes 4931648 | tf_op jit(solution)/shard_map/tbki,bkij->tbj/dot_general | solution.py:77
  73.9 3.1 %collective-permute-start.2 = (bf16[8,128]{1,0:T(8,128)(2,1)S(1)}, bf16[8,128]{1,0:T(8,128)(2,1)S(1)}, u32[]{:S(2)}, u32[]{:S(2)}) collective-permute-start(bf16[8,128]{1,0:T(8,128)(2,1)S(1)} %get-tuple-element.15), channel_id=1, source_target_pairs={{0,4},{4,8},{8,12},{12,16},{16,20},{20,24},{24,28},{1,5},{5,9},{9,... | collective-permute-start | bytes 6152 | tf_op jit(solution)/shard_map/ppermute | solution.py:18
  77.0 1.3 collective-permute-start.3
  78.3 0.0 collective-permute-done.2
  78.3 4.2 %collective-permute-done.3 = bf16[8,128]{1,0:T(8,128)(2,1)S(1)} collective-permute-done((bf16[8,128]{1,0:T(8,128)(2,1)S(1)}, bf16[8,128]{1,0:T(8,128)(2,1)S(1)}, u32[]{:S(2)}, u32[]{:S(2)}) %collective-permute-start.3) | collective-permute-done | bytes 2080 | tf_op jit(solution)/shard_map/ppermute | solution.py:19
  82.5 0.7 gather_fusion.2
  83.2 2.9 %fusion.83 = (bf16[8,4096]{1,0:T(8,128)(2,1)S(1)}, f32[8,4096]{1,0:T(8,128)S(1)}) fusion(f32[8,4096]{1,0:T(8,128)S(1)} %get-tuple-element.20, f32[4096]{0:T(1024)S(1)} %copy-done.3, f32[1,8,32,128]{3,2,1,0:T(8,128)S(1)} %get-tuple-element.7, f32[8]{0:T(128)S(1)} %copy-done.5, bf16[8,32,4,128]{3,0,2,1:T(8,128)(2,1)S(1)} %bitcast.268, ...), kind=kOutput, calls=%fused_computation.129 | convolution fusion | flops 33914880 | bytes 4931648 | tf_op jit(solution)/shard_map/tbki,bkij->tbj/dot_general | solution.py:77
  86.1 2.9 %collective-permute-start.4 = (bf16[8,128]{1,0:T(8,128)(2,1)S(1)}, bf16[8,128]{1,0:T(8,128)(2,1)S(1)}, u32[]{:S(2)}, u32[]{:S(2)}) collective-permute-start(bf16[8,128]{1,0:T(8,128)(2,1)S(1)} %get-tuple-element.13), channel_id=1, source_target_pairs={{0,4},{4,8},{8,12},{12,16},{16,20},{20,24},{24,28},{1,5},{5,9},{9,... | collective-permute-start | bytes 6152 | tf_op jit(solution)/shard_map/ppermute | solution.py:18
  89.0 1.3 collective-permute-start.5
  90.4 4.2 %collective-permute-done.5 = bf16[8,128]{1,0:T(8,128)(2,1)S(1)} collective-permute-done((bf16[8,128]{1,0:T(8,128)(2,1)S(1)}, bf16[8,128]{1,0:T(8,128)(2,1)S(1)}, u32[]{:S(2)}, u32[]{:S(2)}) %collective-permute-start.5) | collective-permute-done | bytes 2080 | tf_op jit(solution)/shard_map/ppermute | solution.py:19
  94.5 0.7 gather_fusion.3
  95.2 0.0 copy-start.4
  95.2 2.9 %fusion.84 = (bf16[8,4096]{1,0:T(8,128)(2,1)S(1)}, f32[8,4096]{1,0:T(8,128)S(1)}) fusion(f32[8,4096]{1,0:T(8,128)S(1)} %get-tuple-element.22, f32[4096]{0:T(1024)S(1)} %copy-done.3, f32[1,8,32,128]{3,2,1,0:T(8,128)S(1)} %get-tuple-element.6, f32[8]{0:T(128)S(1)} %copy-done.5, bf16[8,32,4,128]{3,0,2,1:T(8,128)(2,1)S(1)} %bitcast.269, ...), kind=kOutput, calls=%fused_computation.130 | convolution fusion | flops 33914880 | bytes 4931648 | tf_op jit(solution)/shard_map/tbki,bkij->tbj/dot_general | solution.py:77
  98.2 4.8 %collective-permute-start.6 = (bf16[8,128]{1,0:T(8,128)(2,1)S(1)}, bf16[8,128]{1,0:T(8,128)(2,1)S(1)}, u32[]{:S(2)}, u32[]{:S(2)}) collective-permute-start(bf16[8,128]{1,0:T(8,128)(2,1)S(1)} %get-tuple-element.11), channel_id=1, source_target_pairs={{0,4},{4,8},{8,12},{12,16},{16,20},{20,24},{24,28},{1,5},{5,9},{9,... | collective-permute-start | bytes 6152 | tf_op jit(solution)/shard_map/ppermute | solution.py:18
  103.0 1.3 collective-permute-start.7
  104.3 4.1 %collective-permute-done.7 = bf16[8,128]{1,0:T(8,128)(2,1)S(1)} collective-permute-done((bf16[8,128]{1,0:T(8,128)(2,1)S(1)}, bf16[8,128]{1,0:T(8,128)(2,1)S(1)}, u32[]{:S(2)}, u32[]{:S(2)}) %collective-permute-start.7) | collective-permute-done | bytes 2080 | tf_op jit(solution)/shard_map/ppermute | solution.py:19
  108.5 0.7 gather_fusion.4
  109.2 2.9 %fusion.9 = f32[8,4096]{1,0:T(8,128)S(1)} fusion(f32[8,4096]{1,0:T(8,128)S(1)} %get-tuple-element.24, bf16[8,32,4,128]{3,0,2,1:T(8,128)(2,1)S(1)} %bitcast.267, bf16[32,4,128,128]{3,2,1,0:T(8,128)(2,1)} %all-gather.2.cloned.1.call-done, f32[1,8,32,128]{3,2,1,0:T(8,128)S(1)} %get-tuple-element.5, f32[4096]{0:T(1024)S(1)} %copy-done.3, f32[8]{0:T(128)S(1)} %copy-done.5, ...), kind=kOutput, calls=%fused_computation.18 | convolution fusion | flops 33882112 | bytes 4866112 | tf_op jit(solution)/shard_map/tbki,bkij->tbj/dot_general | solution.py:77
  112.1 0.0 copy-start.2
  112.1 0.6 copy.33
  112.7 0.0 copy-start.7
  112.7 0.0 copy-start.8
  112.7 22.5 %scatter_custom_fusion.2 = f32[33,384]{0,1:T(8,128)S(1)} fusion(s32[4096]{0:T(1024)S(1)} %compare_select_fusion.1, f32[32,4096]{0,1:T(8,128)S(1)} %copy.33, f32[]{:T(128)} %constant.18.clone.1, f32[]{:T(128)} %constant.9.clone.1), kind=kCustom, calls=%fused_computation.54 | custom fusion | flops 135168 | bytes 2147848 | tf_op jit(solution)/shard_map/scatter-add | solution.py:93
  135.2 4.0 %collective-permute-start.8 = (f32[33,128]{0,1:T(8,128)S(1)}, f32[33,128]{0,1:T(8,128)S(1)}, u32[]{:S(2)}, u32[]{:S(2)}) collective-permute-start(f32[33,128]{0,1:T(8,128)S(1)} %get-tuple-element.9), channel_id=1, source_target_pairs={{0,4},{4,8},{8,12},{12,16},{16,20},{20,24},{24,28},{1,5},{5,9},{9,... | collective-permute-start | bytes 50696 | tf_op jit(solution)/shard_map/ppermute | solution.py:18
  139.3 1.3 collective-permute-start.9
  140.6 0.6 collective-permute-done.8
  141.1 4.3 %collective-permute-done.9 = f32[33,128]{0,1:T(8,128)S(1)} collective-permute-done((f32[33,128]{0,1:T(8,128)S(1)}, f32[33,128]{0,1:T(8,128)S(1)}, u32[]{:S(2)}, u32[]{:S(2)}) %collective-permute-start.9) | collective-permute-done | bytes 16928 | tf_op jit(solution)/shard_map/ppermute | solution.py:19
  145.4 0.2 fusion.49
  145.6 0.1 copy.34
  145.7 0.0 copy-done.7
  145.7 0.6 multiply_add_fusion
  (32 shorter events, 0.2 us)
Async XLA Ops:
  7.2 12.9 %copy-start = (bf16[7,8,4096]{2,1,0:T(8,128)(2,1)S(1)}, bf16[7,8,4096]{2,1,0:T(8,128)(2,1)}, u32[]{:S(2)}) copy-start(bf16[7,8,4096]{2,1,0:T(8,128)(2,1)} %param.16) | copy-start | bytes 1376260
  7.2 15.2 %copy-start.10 = (f32[128]{0:T(128)S(1)}, f32[128]{0:T(128)}, u32[]{:S(2)}) copy-start(f32[128]{0:T(128)} %param.26) | copy-start | bytes 1540
  7.2 63.8 %all-gather.2.cloned.1.call-start = ((), (), s32[]{:S(2)}) async-start(), calls=%async_computation.2 | async-start | bytes 5242880 | tf_op jit(solution)/shard_map/all_gather | solution.py:69
  11.3 26.3 %all-to-all-start.1 = ((s32[8,17,1]{1,2,0:T(1,128)}), s32[8,17,1]{1,2,0:T(1,128)S(1)}, u32[]{:S(2)}, u32[]{:S(2)}) async-start(s32[8,17,1]{1,2,0:T(1,128)} %bitcast.12), calls=%async_computation.1 | async-start | bytes 8192 | tf_op jit(solution)/shard_map/all_to_all | solution.py:62
  23.9 19.7 %copy-start.1 = (f32[8,4096]{1,0:T(8,128)S(1)}, f32[8,4096]{1,0:T(8,128)}, u32[]{:S(2)}) copy-start(f32[8,4096]{1,0:T(8,128)} %param.15) | copy-start | bytes 393220
  23.9 25.0 %copy-start.9 = (s32[32,4]{0,1:T(4,128)S(1)}, s32[32,4]{0,1:T(4,128)}, u32[]{:S(2)}) copy-start(s32[32,4]{0,1:T(4,128)} %param.21) | copy-start | bytes 1540
  37.6 32.9 %all-to-all-start = ((bf16[136,4,8,128]{3,2,1,0:T(8,128)(2,1)}), bf16[136,4,8,128]{3,2,1,0:T(8,128)(2,1)S(1)}, u32[]{:S(2)}, u32[]{:S(2)}) async-start(bf16[136,4,8,128]{3,2,1,0:T(8,128)(2,1)} %scatter_fusion), calls=%async_computation | async-start | bytes 2228224 | tf_op jit(solution)/shard_map/all_to_all | solution.py:61
  43.6 27.4 %copy-start.3 = (f32[4096]{0:T(1024)S(1)}, f32[4096]{0:T(1024)}, u32[]{:S(2)}) copy-start(f32[4096]{0:T(1024)} %param.17) | copy-start | bytes 49156
  43.6 27.4 %copy-start.5 = (f32[8]{0:T(128)S(1)}, f32[8]{0:T(128)}, u32[]{:S(2)}) copy-start(f32[8]{0:T(128)} %param.19) | copy-start | bytes 100
  43.6 27.4 %copy-start.6 = (f32[8]{0:T(128)S(1)}, f32[8]{0:T(128)}, u32[]{:S(2)}) copy-start(f32[8]{0:T(128)} %param.18) | copy-start | bytes 100
  43.6 7.2 %collective-permute-start = (bf16[8,128]{1,0:T(8,128)(2,1)S(1)}, bf16[8,128]{1,0:T(8,128)(2,1)S(1)}, u32[]{:S(2)}, u32[]{:S(2)}) collective-permute-start(bf16[8,128]{1,0:T(8,128)(2,1)S(1)} %get-tuple-element.17), channel_id=1, source_target_pairs={{0,4},{4,8},{8,12},{12,16},{16,20},{20,24},{24,28},{1,5},{5,9},{9,... | collective-permute-start | bytes 6152 | tf_op jit(solution)/shard_map/ppermute | solution.py:18
  47.6 5.5 %collective-permute-start.1 = (bf16[8,128]{1,0:T(8,128)(2,1)S(1)}, bf16[8,128]{1,0:T(8,128)(2,1)S(1)}, u32[]{:S(2)}, u32[]{:S(2)}) collective-permute-start(bf16[8,128]{1,0:T(8,128)(2,1)S(1)} %get-tuple-element.18), channel_id=1, source_target_pairs={{4,0},{8,4},{12,8},{16,12},{20,16},{24,20},{28,24},{5,1},{9,5},{13... | collective-permute-start | bytes 6152 | tf_op jit(solution)/shard_map/ppermute | solution.py:19
  73.9 4.4 %collective-permute-start.2 = (bf16[8,128]{1,0:T(8,128)(2,1)S(1)}, bf16[8,128]{1,0:T(8,128)(2,1)S(1)}, u32[]{:S(2)}, u32[]{:S(2)}) collective-permute-start(bf16[8,128]{1,0:T(8,128)(2,1)S(1)} %get-tuple-element.15), channel_id=1, source_target_pairs={{0,4},{4,8},{8,12},{12,16},{16,20},{20,24},{24,28},{1,5},{5,9},{9,... | collective-permute-start | bytes 6152 | tf_op jit(solution)/shard_map/ppermute | solution.py:18
  77.0 5.5 %collective-permute-start.3 = (bf16[8,128]{1,0:T(8,128)(2,1)S(1)}, bf16[8,128]{1,0:T(8,128)(2,1)S(1)}, u32[]{:S(2)}, u32[]{:S(2)}) collective-permute-start(bf16[8,128]{1,0:T(8,128)(2,1)S(1)} %get-tuple-element.16), channel_id=1, source_target_pairs={{4,0},{8,4},{12,8},{16,12},{20,16},{24,20},{28,24},{5,1},{9,5},{13... | collective-permute-start | bytes 6152 | tf_op jit(solution)/shard_map/ppermute | solution.py:19
  86.1 4.3 %collective-permute-start.4 = (bf16[8,128]{1,0:T(8,128)(2,1)S(1)}, bf16[8,128]{1,0:T(8,128)(2,1)S(1)}, u32[]{:S(2)}, u32[]{:S(2)}) collective-permute-start(bf16[8,128]{1,0:T(8,128)(2,1)S(1)} %get-tuple-element.13), channel_id=1, source_target_pairs={{0,4},{4,8},{8,12},{12,16},{16,20},{20,24},{24,28},{1,5},{5,9},{9,... | collective-permute-start | bytes 6152 | tf_op jit(solution)/shard_map/ppermute | solution.py:18
  89.0 5.5 %collective-permute-start.5 = (bf16[8,128]{1,0:T(8,128)(2,1)S(1)}, bf16[8,128]{1,0:T(8,128)(2,1)S(1)}, u32[]{:S(2)}, u32[]{:S(2)}) collective-permute-start(bf16[8,128]{1,0:T(8,128)(2,1)S(1)} %get-tuple-element.14), channel_id=1, source_target_pairs={{4,0},{8,4},{12,8},{16,12},{20,16},{24,20},{28,24},{5,1},{9,5},{13... | collective-permute-start | bytes 6152 | tf_op jit(solution)/shard_map/ppermute | solution.py:19
  95.2 9.1 %copy-start.4 = (s32[4096]{0:T(1024)S(1)}, s32[4096]{0:T(1024)}, u32[]{:S(2)}) copy-start(s32[4096]{0:T(1024)} %param.27) | copy-start | bytes 49156
  98.2 6.2 %collective-permute-start.6 = (bf16[8,128]{1,0:T(8,128)(2,1)S(1)}, bf16[8,128]{1,0:T(8,128)(2,1)S(1)}, u32[]{:S(2)}, u32[]{:S(2)}) collective-permute-start(bf16[8,128]{1,0:T(8,128)(2,1)S(1)} %get-tuple-element.11), channel_id=1, source_target_pairs={{0,4},{4,8},{8,12},{12,16},{16,20},{20,24},{24,28},{1,5},{5,9},{9,... | collective-permute-start | bytes 6152 | tf_op jit(solution)/shard_map/ppermute | solution.py:18
  103.0 5.5 %collective-permute-start.7 = (bf16[8,128]{1,0:T(8,128)(2,1)S(1)}, bf16[8,128]{1,0:T(8,128)(2,1)S(1)}, u32[]{:S(2)}, u32[]{:S(2)}) collective-permute-start(bf16[8,128]{1,0:T(8,128)(2,1)S(1)} %get-tuple-element.12), channel_id=1, source_target_pairs={{4,0},{8,4},{12,8},{16,12},{20,16},{24,20},{28,24},{5,1},{9,5},{13... | collective-permute-start | bytes 6152 | tf_op jit(solution)/shard_map/ppermute | solution.py:19
  112.1 23.1 %copy-start.2 = (f32[8,4096]{1,0:T(8,128)}, f32[8,4096]{1,0:T(8,128)S(1)}, u32[]{:S(2)}) copy-start(f32[8,4096]{1,0:T(8,128)S(1)} %fusion.9) | copy-start | bytes 393220
  112.7 33.0 %copy-start.7 = (f32[8,128]{1,0:T(8,128)S(1)}, f32[8,128]{1,0:T(8,128)}, u32[]{:S(2)}) copy-start(f32[8,128]{1,0:T(8,128)} %param.29) | copy-start | bytes 12292
  112.7 33.0 %copy-start.8 = (f32[8,128]{1,0:T(8,128)S(1)}, f32[8,128]{1,0:T(8,128)}, u32[]{:S(2)}) copy-start(f32[8,128]{1,0:T(8,128)} %param.28) | copy-start | bytes 12292
  135.2 5.9 %collective-permute-start.8 = (f32[33,128]{0,1:T(8,128)S(1)}, f32[33,128]{0,1:T(8,128)S(1)}, u32[]{:S(2)}, u32[]{:S(2)}) collective-permute-start(f32[33,128]{0,1:T(8,128)S(1)} %get-tuple-element.9), channel_id=1, source_target_pairs={{0,4},{4,8},{8,12},{12,16},{16,20},{20,24},{24,28},{1,5},{5,9},{9,... | collective-permute-start | bytes 50696 | tf_op jit(solution)/shard_map/ppermute | solution.py:18
  139.3 6.2 %collective-permute-start.9 = (f32[33,128]{0,1:T(8,128)S(1)}, f32[33,128]{0,1:T(8,128)S(1)}, u32[]{:S(2)}, u32[]{:S(2)}) collective-permute-start(f32[33,128]{0,1:T(8,128)S(1)} %get-tuple-element.10), channel_id=1, source_target_pairs={{4,0},{8,4},{12,8},{16,12},{20,16},{24,20},{28,24},{5,1},{9,5},{13... | collective-permute-start | bytes 50696 | tf_op jit(solution)/shard_map/ppermute | solution.py:19
Sparse Core Ops, SparseCore 0:
  9.6 37.1 all-gather.1
where the time goes:
time: 154 us; the launch traced here: 153 us
  starting transfers between devices  38.5 us (25%)
  waiting for transfers between devices  37.5 us (24%)
  other arithmetic  27.3 us (18%)
  local copies, waits for them, and re-layouts  23.4 us (15%)
  between operations  14.5 us (9%)
  matrix products  12 us (8%)
    scatter-add x1, other arithmetic, shards(): partial_value = jnp.zeros((values.shape[0], 3 * voxels_here), jnp.float32...  22.5 us
    ppermute x5, waiting for transfers between devices, extended_2(): after = lax.ppermute(leading, axis, down)  19 us
    ppermute x5, starting transfers between devices, extended_2(): before = lax.ppermute(last, axis, up)  18.8 us
    all_to_all x1, waiting for transfers between devices, shards(): lax.all_to_all(send_rates, 'patch', split_axis=0, concat_axis=0, tiled=True)  16.7 us
    scatter x1, local copies, waits for them, and re-layouts, shards(): jnp.zeros((slots, STEPS, trials_here, BLOCK), jnp.bfloat16).at[slot]  13.7 us
    dot_general x4, matrix products, shards(): jnp.einsum('tbki,bkij->tbj', picked, tiles, preferred_element_type=jnp.fl...  11.6 us
    all_to_all x1, starting transfers between devices, shards(): lax.all_to_all(send_blocks, 'patch', split_axis=0, concat_axis=0, tiled=T...  7.28 us
    ppermute x5, starting transfers between devices, extended_2(): after = lax.ppermute(leading, axis, down)  6.46 us
  transfers between devices with their start and end apart: 13, of which 8 were waited for; matrix products, arithmetic and copies ran while one was open for 16% of the time, Pallas kernels for 0%

commit v1 on v0

--- a/solution.py
+++ b/solution.py
@@ -1,11 +1,17 @@
+import functools
+
 import jax
 import jax.numpy as jnp
 from jax import lax
+from jax.experimental import pallas as pl
+from jax.experimental.pallas import tpu as pltpu
 from jax.sharding import PartitionSpec as P
 
 BLOCK = 128
 STEPS = 4
 HIST = 7
+CHUNKS = 4
+MESH = pl.DeviceIdType.MESH
 
 
 def extended_2(array, sides, width):
@@ -108,6 +114,537 @@
     return (rate, vaso, flow)
 
 
+def window(
+    patches,
+    groups,
+    act_ref,
+    hist_ref,
+    drive_ref,
+    slope_ref,
+    strength_ref,
+    kern_ref,
+    index_ref,
+    source_ref,
+    delay_ref,
+    target_ref,
+    block_ref,
+    weight_ref,
+    owner_ref,
+    vaso_ref,
+    flow_ref,
+    act_out,
+    vaso_out,
+    flow_out,
+    ht,
+    hist2,
+    send,
+    recv,
+    over_f,
+    over_send,
+    over_recv,
+    meta_send,
+    meta_recv,
+    tiles,
+    ext,
+    halo_send,
+    halo,
+    coupling,
+    owned,
+    vox_send,
+    vox,
+    send_sem,
+    recv_sem,
+    osend_sem,
+    orecv_sem,
+    msend_sem,
+    mrecv_sem,
+    xsend_sem,
+    xrecv_sem,
+    rsend_sem,
+    rrecv_sem,
+    csem,
+    hsend_sem,
+    hrecv_sem,
+    vsend_sem,
+    vrecv_sem,
+    local_sem,
+):
+    f32, bf16, i32 = jnp.float32, jnp.bfloat16, jnp.int32
+    n = patches
+    nblk = 32
+    me = lax.axis_index("patch")
+    grp = lax.axis_index("trial")
+    far = lax.rem(grp + 2, groups)
+    near = grp + 1 - 2 * lax.rem(grp, 2)
+
+    barrier = pltpu.get_barrier_semaphore()
+    for d in range(1, n):
+        pl.semaphore_signal(
+            barrier, inc=1, device_id={"patch": lax.rem(me + d, n)}, device_id_type=MESH
+        )
+    for g in (far, near):
+        pl.semaphore_signal(barrier, inc=1, device_id={"trial": g}, device_id_type=MESH)
+
+    def remote(src, dst, ssem, rsem, where):
+        return pltpu.make_async_remote_copy(
+            src_ref=src,
+            dst_ref=dst,
+            send_sem=ssem,
+            recv_sem=rsem,
+            device_id=where,
+            device_id_type=MESH,
+        )
+
+    def part(c):
+        return pl.ds(c * (nblk // CHUNKS), nblk // CHUNKS)
+
+    own_tiles = pltpu.make_async_copy(kern_ref, tiles.at[grp], local_sem)
+    own_tiles.start()
+
+    def tile_far(k, c):
+        return remote(
+            kern_ref.at[part(c)],
+            tiles.at[k, part(c)],
+            xsend_sem.at[c],
+            xrecv_sem.at[c],
+            {"trial": far},
+        )
+
+    def tile_near(k):
+        return remote(kern_ref, tiles.at[k], csem.at[0], csem.at[1], {"trial": near})
+
+    def tile_relay(k, c):
+        return remote(
+            tiles.at[k, part(c)],
+            tiles.at[k, part(c)],
+            rsend_sem.at[c],
+            rrecv_sem.at[c],
+            {"trial": near},
+        )
+
+    def main_copy(s, p, q):
+        return remote(
+            send.at[s, pl.ds(pl.multiple_of(q * 16, 16), 16)],
+            recv.at[s, pl.ds(pl.multiple_of(p * 16, 16), 16)],
+            send_sem.at[s, q],
+            recv_sem.at[s, p],
+            {"patch": q},
+        )
+
+    def over_copy(p, q):
+        return remote(
+            over_send.at[q], over_recv.at[p], osend_sem.at[q], orecv_sem.at[p], {"patch": q}
+        )
+
+    def meta_copy(p, q):
+        return remote(
+            meta_send.at[q], meta_recv.at[p], msend_sem.at[q], mrecv_sem.at[p], {"patch": q}
+        )
+
+    def halo_copy(s, side):
+        where = me + 1 if side == 0 else me - 1
+        return remote(
+            halo_send.at[s, side],
+            halo.at[s, side],
+            hsend_sem.at[s, side],
+            hrecv_sem.at[s, side],
+            {"patch": where},
+        )
+
+    def vox_copy(side):
+        where = me + 1 if side == 0 else me - 1
+        return remote(
+            vox_send.at[side], vox.at[side], vsend_sem.at[side], vrecv_sem.at[side], {"patch": where}
+        )
+
+    has_left, has_right = me > 0, me < n - 1
+
+    def halo_start(s):
+        halo_send[s, 0] = ext[s, nblk]
+        halo_send[s, 1] = ext[s, 1]
+
+        @pl.when(has_right)
+        def _():
+            halo_copy(s, 0).start()
+
+        @pl.when(has_left)
+        def _():
+            halo_copy(s, 1).start()
+
+    def halo_take(s):
+        @pl.when(has_left)
+        def _():
+            halo_copy(s, 0).wait_recv()
+            ext[s, 0] = halo[s, 0]
+
+        @pl.when(has_right)
+        def _():
+            halo_copy(s, 1).wait_recv()
+            ext[s, nblk + 1] = halo[s, 1]
+
+    sub = lax.broadcasted_iota(i32, (128, 128), 0)
+    lane = lax.broadcasted_iota(i32, (128, 128), 1)
+    eye = sub == lane
+
+    def row_of(col):
+        return jnp.sum(jnp.where(eye, col, 0.0), axis=0, keepdims=True)
+
+    target_col = jnp.broadcast_to(target_ref[...].astype(f32), (128, 128))
+    target_row = row_of(target_col)
+    same = target_col == target_row
+    rank_row = jnp.sum(jnp.where(same & (sub < lane), 1.0, 0.0), axis=0, keepdims=True)
+    rank_col = jnp.sum(jnp.where(same & (lane < sub), 1.0, 0.0), axis=1, keepdims=True)
+    key_row = ((delay_ref[...] - 1) * nblk + source_ref[...]).astype(f32)
+    weight_row = weight_ref[...]
+    slot_row = jnp.where(rank_row < 16.0, target_row * 16.0 + rank_row, -1.0)
+    sel = sub.astype(f32) == slot_row
+    q8 = lax.broadcasted_iota(i32, (n, 128), 0).astype(f32)
+    sel_over = (q8 == target_row) & (rank_row == 16.0)
+
+    def pick(mask, row):
+        return jnp.sum(jnp.where(mask, row, 0.0), axis=1, keepdims=True)
+
+    key = pick(sel, key_row)
+    weight = pick(sel, weight_row)
+    key_over = pick(sel_over, key_row)
+    weight_over = pick(sel_over, weight_row)
+
+    def turn(lag, _):
+        old = hist_ref[lag].astype(f32)
+        for b in range(nblk):
+            ht[lag, pl.ds(b, 8, stride=nblk), :] = old[:, b * 128 : (b + 1) * 128]
+        rows = pl.ds(pl.multiple_of(lag * nblk, nblk), nblk)
+        for j in range(8):
+            hist2[rows, j * 128 : (j + 1) * 128] = ht[lag, j * nblk : (j + 1) * nblk, :].astype(bf16)
+        return 0
+
+    lax.fori_loop(0, HIST, turn, 0)
+    hist2[HIST * nblk :, :] = jnp.zeros((nblk, 1024), bf16)
+
+    wide = lax.broadcasted_iota(i32, (128, 256), 1).astype(f32)
+    wide8 = lax.broadcasted_iota(i32, (n, 256), 1).astype(f32)
+
+    def gathered(s):
+        choose = jnp.where(wide == key - float(s * nblk), 1.0, 0.0).astype(bf16)
+        rows = jnp.dot(choose, hist2[...], preferred_element_type=f32)
+        send[s] = (rows * weight).astype(bf16)
+
+    gathered(0)
+
+    a = jnp.where(q8 == target_row, block_ref[...].astype(f32), 0.0).astype(bf16)
+    lanes = lane.astype(f32)
+    mef = me.astype(f32)
+    b1 = jnp.where((rank_col < 16.0) & (lanes == rank_col + mef * 16.0), 1.0, 0.0).astype(bf16)
+    b2 = jnp.where((rank_col == 16.0) & (lanes == mef), 1.0, 0.0).astype(bf16)
+    m1 = jnp.dot(a, b1, preferred_element_type=f32)
+    m2 = jnp.dot(a, b2, preferred_element_type=f32)
+    m = jnp.concatenate([m1, m2], axis=1)
+    for q in range(n):
+        meta_send[q] = jnp.broadcast_to(m[q : q + 1], (8, 256))
+
+    for b in range(nblk):
+        ext[0, b + 1] = act_ref[:, b * 128 : (b + 1) * 128]
+    for s in range(STEPS):
+        ext[s, 0] = jnp.zeros((8, 128), f32)
+        ext[s, nblk + 1] = jnp.zeros((8, 128), f32)
+
+    pl.semaphore_wait(barrier, n + 1)
+    for c in range(CHUNKS):
+        tile_far(grp, c).start()
+    for d in range(1, n):
+        main_copy(0, me, lax.rem(me + d, n)).start()
+    tile_near(grp).start()
+    halo_start(0)
+    for d in range(1, n):
+        meta_copy(me, lax.rem(me + d, n)).start()
+    for s in range(1, STEPS):
+        gathered(s)
+        for d in range(1, n):
+            main_copy(s, me, lax.rem(me + d, n)).start()
+        if s == 1:
+            choose = jnp.concatenate(
+                [jnp.where(wide8 == key_over - float(t * nblk), 1.0, 0.0) for t in range(STEPS)],
+                axis=0,
+            ).astype(bf16)
+            rows = jnp.dot(choose, hist2[...], preferred_element_type=f32)
+            for t in range(STEPS):
+                for j in range(8):
+                    over_f[pl.ds(t * 8 + j, n, stride=32), :] = (
+                        rows[t * 8 : t * 8 + 8, j * 128 : (j + 1) * 128] * weight_over
+                    )
+            for q in range(n):
+                over_send[q] = over_f[q * 32 : (q + 1) * 32, :].astype(bf16)
+            for d in range(1, n):
+                over_copy(me, lax.rem(me + d, n)).start()
+
+    mine16 = pl.ds(pl.multiple_of(me * 16, 16), 16)
+    for s in range(STEPS):
+        recv[s, mine16, :] = send[s, mine16, :]
+    over_recv[me] = over_send[me]
+    meta_recv[me] = meta_send[me]
+
+    first = ((me - 1) * 128).astype(f32)
+    vox_id = lax.broadcasted_iota(i32, (384, 128), 0).astype(f32) + first
+
+    def member(b, _):
+        owner = owner_ref[pl.ds(b, 1), :].astype(f32)
+        owned[b] = jnp.where(vox_id == owner, 1.0, 0.0).astype(bf16)
+        return 0
+
+    lax.fori_loop(0, nblk, member, 0)
+
+    eye8 = lax.broadcasted_iota(i32, (8, 8), 0) == lax.broadcasted_iota(i32, (8, 8), 1)
+    slope = jnp.sum(jnp.where(eye8, slope_ref[...], 0.0), axis=1, keepdims=True)
+    strength = jnp.sum(jnp.where(eye8, strength_ref[...], 0.0), axis=1, keepdims=True)
+    slope = jnp.broadcast_to(slope, (8, 128))
+    strength = jnp.broadcast_to(strength, (8, 128))
+
+    for d in range(1, n):
+        p = lax.rem(me + d, n)
+        meta_copy(p, me).wait_recv()
+        over_copy(p, me).wait_recv()
+    where_row = meta_recv[0]
+    for p in range(1, n):
+        where_row = where_row + meta_recv[p]
+    where_row = where_row[0:1, 0:144]
+    onehot = jnp.where(
+        lax.broadcasted_iota(i32, (nblk, 144), 0).astype(f32) == where_row, 1.0, 0.0
+    ).astype(bf16)
+    for p in range(n):
+        over_f[p * 32 : (p + 1) * 32, :] = over_recv[p].astype(f32)
+    for s in range(STEPS):
+        extra = jnp.concatenate(
+            [over_f[pl.ds(s * 8 + j, n, stride=32), :] for j in range(8)], axis=1
+        )
+        recv[s, 128:144, :] = jnp.concatenate([extra, jnp.zeros_like(extra)], axis=0).astype(bf16)
+
+    def couple(s):
+        for d in range(1, n):
+            main_copy(s, lax.rem(me + d, n), me).wait_recv()
+        total = jnp.dot(onehot, recv[s], preferred_element_type=f32)
+        for j in range(8):
+            coupling[s, j * nblk : (j + 1) * nblk, :] = total[:, j * 128 : (j + 1) * 128]
+
+    def update(s, b):
+        lhs = jnp.concatenate([ext[s, index_ref[b, k]] for k in range(4)], axis=1).astype(bf16)
+        rhs = jnp.concatenate([tiles[k, b] for k in range(4)], axis=0)
+        local = jnp.dot(lhs, rhs, preferred_element_type=f32)
+        tract = coupling[s, pl.ds(b, 8, stride=nblk), :]
+        pre = slope * (local + strength * tract + drive_ref[pl.ds(b, 1), :])
+        rate = ext[s, b + 1]
+        ext[s + 1, b + 1] = rate + 0.5 * (jax.nn.sigmoid(pre) - rate)
+
+    def updates(s, low, high, width):
+        def some(i, _):
+            for u in range(width):
+                update(s, low + i * width + u)
+            return 0
+
+        lax.fori_loop(0, (high - low) // width, some, 0)
+
+    couple(0)
+    halo_take(0)
+    own_tiles.wait()
+    tile_near(near).wait_recv()
+    tile_far(far, 0).wait_recv()
+    tile_relay(far, 0).start()
+    other = lax.rem(near + 2, groups)
+    for c in range(CHUNKS):
+        if c + 1 < CHUNKS:
+            tile_far(far, c + 1).wait_recv()
+            tile_relay(far, c + 1).start()
+        tile_relay(other, c).wait_recv()
+        updates(0, c * (nblk // CHUNKS), (c + 1) * (nblk // CHUNKS), nblk // CHUNKS)
+    halo_start(1)
+
+    for s in range(1, STEPS):
+        couple(s)
+        updates(s, 1, nblk - 1, 10)
+        halo_take(s)
+        update(s, 0)
+        update(s, nblk - 1)
+        if s + 1 < STEPS:
+            halo_start(s + 1)
+
+    ones = jnp.ones((16, 512), bf16)
+
+    def sums(i, total):
+        rates = [
+            jnp.concatenate([ext[s + 1, i * 4 + u + 1] for u in range(4)], axis=1)
+            for s in range(STEPS)
+        ]
+        rates = jnp.concatenate(rates, axis=0)
+        high = rates.astype(bf16)
+        low = (rates - high.astype(f32)).astype(bf16)
+        lhs = jnp.concatenate([high, low, ones], axis=0)
+        rhs = jnp.concatenate([owned[i * 4 + u] for u in range(4)], axis=1)
+        return total + lax.dot_general(
+            lhs, rhs, (((1,), (1,)), ((), ())), preferred_element_type=f32
+        )
+
+    total = lax.fori_loop(0, nblk // 4, sums, jnp.zeros((80, 384), f32))
+    total = jnp.concatenate([total[0:32] + total[32:64], total[64:72]], axis=0)
+    vox_send[0] = total[:, 256:384]
+    vox_send[1] = total[:, 0:128]
+
+    @pl.when(has_right)
+    def _():
+        vox_copy(0).start()
+
+    @pl.when(has_left)
+    def _():
+        vox_copy(1).start()
+
+    vox_send[2] = total[:, 128:256]
+    for b in range(nblk):
+        act_out[:, b * 128 : (b + 1) * 128] = ext[STEPS, b + 1]
+
+    @pl.when(has_left)
+    def _():
+        vox_copy(0).wait_recv()
+        vox_send[2] = vox_send[2] + vox[0]
+
+    @pl.when(has_right)
+    def _():
+        vox_copy(1).wait_recv()
+        vox_send[2] = vox_send[2] + vox[1]
+
+    floor = jnp.maximum(vox_send[2, 32:40, :], 1.0)
+    vaso = vaso_ref[...]
+    flow = flow_ref[...]
+    for s in range(STEPS):
+        level = vox_send[2, s * 8 : s * 8 + 8, :] / floor
+        vaso = vaso + 0.5 * (level - 0.65 * vaso - 0.41 * (flow - 1.0))
+        flow = flow + 0.5 * vaso
+    vaso_out[...] = vaso
+    flow_out[...] = flow
+
+    for d in range(1, n):
+        q = lax.rem(me + d, n)
+        for s in range(STEPS):
+            main_copy(s, me, q).wait_send()
+        over_copy(me, q).wait_send()
+        meta_copy(me, q).wait_send()
+    tile_near(grp).wait_send()
+    for c in range(CHUNKS):
+        tile_far(grp, c).wait_send()
+        tile_relay(far, c).wait_send()
+
+    @pl.when(has_right)
+    def _():
+        for s in range(STEPS):
+            halo_copy(s, 0).wait_send()
+        vox_copy(0).wait_send()
+
+    @pl.when(has_left)
+    def _():
+        for s in range(STEPS):
+            halo_copy(s, 1).wait_send()
+        vox_copy(1).wait_send()
+
+
+def fused(
+    activity,
+    history,
+    drive,
+    slope,
+    strength,
+    kernel,
+    kernel_index,
+    tract_source,
+    tract_delay,
+    tract_target,
+    tract_block,
+    tract_weight,
+    voxel_owner,
+    vaso_signal,
+    blood_flow,
+):
+    n, groups = lax.axis_size("patch"), lax.axis_size("trial")
+    f32, bf16 = jnp.float32, jnp.bfloat16
+    vmem = pl.BlockSpec(memory_space=pltpu.VMEM)
+    smem = pl.BlockSpec(memory_space=pltpu.SMEM)
+    dma = pltpu.SemaphoreType.DMA
+    scratch = [
+        pltpu.VMEM((HIST, 256, 128), f32),
+        pltpu.VMEM((256, 1024), bf16),
+        pltpu.VMEM((STEPS, 128, 1024), bf16),
+        pltpu.VMEM((STEPS, 144, 1024), bf16),
+        pltpu.VMEM((256, 128), f32),
+        pltpu.VMEM((n, 32, 128), bf16),
+        pltpu.VMEM((n, 32, 128), bf16),
+        pltpu.VMEM((n, 8, 256), f32),
+        pltpu.VMEM((n, 8, 256), f32),
+        pltpu.VMEM((4, 32, 128, 128), bf16),
+        pltpu.VMEM((STEPS + 1, 34, 8, 128), f32),
+        pltpu.VMEM((STEPS, 2, 8, 128), f32),
+        pltpu.VMEM((STEPS, 2, 8, 128), f32),
+        pltpu.VMEM((STEPS, 256, 128), f32),
+        pltpu.VMEM((32, 384, 128), bf16),
+        pltpu.VMEM((3, 40, 128), f32),
+        pltpu.VMEM((2, 40, 128), f32),
+        dma((STEPS, n)),
+        dma((STEPS, n)),
+        dma((n,)),
+        dma((n,)),
+        dma((n,)),
+        dma((n,)),
+        dma((CHUNKS,)),
+        dma((CHUNKS,)),
+        dma((CHUNKS,)),
+        dma((CHUNKS,)),
+        dma((2,)),
+        dma((STEPS, 2)),
+        dma((STEPS, 2)),
+        dma((2,)),
+        dma((2,)),
+        dma,
+    ]
+    return pl.pallas_call(
+        functools.partial(window, n, groups),
+        out_shape=(
+            jax.ShapeDtypeStruct(activity.shape, f32),
+            jax.ShapeDtypeStruct(vaso_signal.shape, f32),
+            jax.ShapeDtypeStruct(blood_flow.shape, f32),
+        ),
+        in_specs=[vmem] * 6 + [smem] + [vmem] * 8,
+        out_specs=(vmem, vmem, vmem),
+        scratch_shapes=scratch,
+        compiler_params=pltpu.CompilerParams(
+            collective_id=0, has_side_effects=True, vmem_limit_bytes=40 * 1024 * 1024
+        ),
+    )(
+        activity,
+        history,
+        drive.reshape(32, 128),
+        slope.reshape(1, 8),
+        strength.reshape(1, 8),
+        kernel.reshape(32, 128, 128),
+        kernel_index,
+        tract_source.reshape(1, 128),
+        tract_delay.reshape(1, 128),
+        tract_target,
+        tract_block.reshape(1, 128),
+        tract_weight.reshape(1, 128),
+        voxel_owner.reshape(32, 128),
+        vaso_signal,
+        blood_flow,
+    )
+
+
+def planned(*args):
+    shapes = (
+        lax.axis_size("patch"),
+        lax.axis_size("trial"),
+        args[0].shape,
+        args[7].shape,
+        args[13].shape,
+    )
+    if shapes == (8, 4, (8, 4096), (128,), (8, 128)):
+        return fused(*args)
+    return shards(*args)
+
+
 def solution(mesh):
     placed = (
         P("trial", "patch"),
@@ -127,7 +664,7 @@
         P("trial", "patch"),
     )
     return jax.shard_map(
-        shards,
+        planned,
         mesh=mesh,
         in_specs=placed,
         out_specs=(P("trial", "patch"), P("trial", "patch"), P("trial", "patch")),

time: 154 us -> 61.8 us (0.40)
  Pallas kernels: 0 us -> 53.7 us
  starting transfers between devices: 38.5 us -> 0 us
  waiting for transfers between devices: 37.5 us -> 0 us
  other arithmetic: 27.3 us -> 0 us
  local copies, waits for them, and re-layouts: 23.4 us -> 7.05 us
  between operations: 14.5 us -> 0.72 us
  matrix products: 12 us -> 0 us
    pallas_call x0 -> x1, Pallas kernels: none -> 53.7 us  [fused(): pl.pallas_call(functools.partial(window, n, groups), out_shape=(jax.Shape...]
    ppermute x10 -> x0, starting transfers between devices: 25.2 us -> none  [the longest x5 18.8 us: extended_2(): before = lax.ppermute(last, axis, up)]
    scatter-add x1 -> x0, other arithmetic: 22.5 us -> none  [shards(): partial_value = jnp.zeros((values.shape[0], 3 * voxels_here), jnp.float32...]
    ppermute x10 -> x0, waiting for transfers between devices: 20 us -> none  [the longest x5 19 us: extended_2(): after = lax.ppermute(leading, axis, down)]
    all_to_all x2 -> x0, waiting for transfers between devices: 16.7 us -> none  [the longest x1 16.7 us: shards(): lax.all_to_all(send_rates, 'patch', split_axis=0, concat_axis=0, tiled=True)]
    scatter x2 -> x0, local copies, waits for them, and re-layouts: 14.8 us -> none  [the longest x1 13.7 us: shards(): jnp.zeros((slots, STEPS, trials_here, BLOCK), jnp.bfloat16).at[slot]]
    all_to_all x2 -> x0, starting transfers between devices: 13.2 us -> none  [the longest x1 7.28 us: shards(): lax.all_to_all(send_blocks, 'patch', split_axis=0, concat_axis=0, tiled=T...]
    dot_general x5 -> x0, matrix products: 12 us -> none  [the longest x4 11.6 us: shards(): jnp.einsum('tbki,bkij->tbj', picked, tiles, preferred_element_type=jnp.fl...]
  transfers between devices with their start and end apart: 13 -> 0, of which waited for: 8 -> 0; matrix products, arithmetic and copies ran while one was open for 16% -> 0% of each run, Pallas kernels for 0% -> 0%
where the time goes in v1:
time: 61.8 us; the launch traced here: 61.5 us
  Pallas kernels  53.7 us (87%)
  local copies, waits for them, and re-layouts  7.05 us (11%)
  between operations  0.72 us (1%)
    pallas_call x1, Pallas kernels, fused(): pl.pallas_call(functools.partial(window, n, groups), out_shape=(jax.Shape...  53.7 us
    unnamed x35, local copies, waits for them, and re-layouts  7.05 us

profile of v1, /device:TPU:0, one launch (start us, length us, event | category | flops | bytes accessed | tf_op | source)
XLA Modules:
  0.0 61.5 jit_solution(7584892653692636113)
XLA Ops:
  0.6 0.0 copy-start.13
  0.6 0.7 %copy-done.13 = s32[32,4]{0,1:T(4,128)S(1)} copy-done((s32[32,4]{0,1:T(4,128)S(1)}, s32[32,4]{0,1:T(4,128)}, u32[]{:S(2)}) %copy-start.13) | copy-done | bytes 536
  1.3 0.0 copy-start.14
  1.3 0.1 copy.18.index_ref
  1.4 0.6 copy-done.14
  2.0 0.0 copy-start.3
  2.0 0.0 copy-start.4
  2.0 0.0 copy-start.5
  2.0 0.0 copy-start.6
  2.0 0.0 copy-start.7
  2.0 0.0 copy-start.8
  2.0 0.0 copy-start.9
  2.0 0.0 copy-start.10
  2.0 0.0 copy-start.11
  2.0 0.0 copy-start.12
  2.1 0.1 copy.19.target_ref
  2.2 0.5 copy-done.3
  2.7 0.0 copy-done.4
  2.7 0.0 copy-done.5
  2.7 0.0 copy-done.6
  2.7 0.0 copy-done.7
  2.7 0.0 copy-done.8
  2.7 0.0 copy-done.9
  2.7 0.0 copy-done.10
  2.7 0.0 copy-done.11
  2.8 0.0 copy-done.12
  2.8 0.0 copy-start
  2.8 1.2 %copy-done = bf16[32,1,128,128]{3,2,1,0:T(8,128)(2,1)S(1)} copy-done((bf16[32,1,128,128]{3,2,1,0:T(8,128)(2,1)S(1)}, bf16[32,1,128,128]{3,2,1,0:T(8,128)(2,1)}, u32[]{:S(2)}) %copy-start) | copy-done | bytes 1048600
  4.0 0.0 copy-start.1
  4.0 1.0 %copy-done.1 = bf16[7,8,4096]{2,1,0:T(8,128)(2,1)S(1)} copy-done((bf16[7,8,4096]{2,1,0:T(8,128)(2,1)S(1)}, bf16[7,8,4096]{2,1,0:T(8,128)(2,1)}, u32[]{:S(2)}) %copy-start.1) | copy-done | bytes 458776
  5.0 0.0 copy-start.2
  5.0 0.9 %copy-done.2 = f32[8,4096]{1,0:T(8,128)S(1)} copy-done((f32[8,4096]{1,0:T(8,128)S(1)}, f32[8,4096]{1,0:T(8,128)}, u32[]{:S(2)}) %copy-start.2) | copy-done | bytes 131096
  5.9 53.7 %shard_map.166 = (f32[8,4096]{1,0:T(8,128)S(1)}, f32[8,128]{1,0:T(8,128)S(1)}, f32[8,128]{1,0:T(8,128)S(1)}) custom-call(f32[8,4096]{1,0:T(8,128)S(1)} %copy-done.2, bf16[7,8,4096]{2,1,0:T(8,128)(2,1)S(1)} %copy-done.1, f32[32,128]{1,0:T(8,128)S(1)} %bitcast.10, f32[1,8]{1,0:T(1,128)S(1)} %bitcast.12, f32[1,8]{1,0:T(1,128)S(1)} %bitcast.13, ...), custom_call_target="tpu_custom_call" | custom-call | tf_op jit(solution)/shard_map/pallas_call | solution.py:603
  59.7 0.7 %copy.23 = f32[8,4096]{1,0:T(8,128)} copy(f32[8,4096]{1,0:T(8,128)S(1)} %get-tuple-element.6) | data formatting | bytes 262144
  60.3 0.6 copy.24
  60.9 0.6 copy.25
Async XLA Ops:
  0.6 0.7 %copy-start.13 = (s32[32,4]{0,1:T(4,128)S(1)}, s32[32,4]{0,1:T(4,128)}, u32[]{:S(2)}) copy-start(s32[32,4]{0,1:T(4,128)} %param.21) | copy-start | bytes 1540
  1.3 0.7 %copy-start.14 = (s32[128,1]{0,1:T(1,128)S(1)}, s32[128,1]{0,1:T(1,128)}, u32[]{:S(2)}) copy-start(s32[128,1]{0,1:T(1,128)} %param.24) | copy-start | bytes 1540
  2.0 0.7 %copy-start.3 = (f32[4096]{0:T(1024)S(1)}, f32[4096]{0:T(1024)}, u32[]{:S(2)}) copy-start(f32[4096]{0:T(1024)} %param.17) | copy-start | bytes 49156
  2.0 0.7 %copy-start.4 = (s32[4096]{0:T(1024)S(1)}, s32[4096]{0:T(1024)}, u32[]{:S(2)}) copy-start(s32[4096]{0:T(1024)} %param.27) | copy-start | bytes 49156
  2.0 0.7 %copy-start.5 = (f32[8,128]{1,0:T(8,128)S(1)}, f32[8,128]{1,0:T(8,128)}, u32[]{:S(2)}) copy-start(f32[8,128]{1,0:T(8,128)} %vaso_ref.1) | copy-start | bytes 12292
  2.0 0.7 %copy-start.6 = (f32[8,128]{1,0:T(8,128)S(1)}, f32[8,128]{1,0:T(8,128)}, u32[]{:S(2)}) copy-start(f32[8,128]{1,0:T(8,128)} %flow_ref.1) | copy-start | bytes 12292
  2.0 0.7 %copy-start.7 = (f32[8]{0:T(128)S(1)}, f32[8]{0:T(128)}, u32[]{:S(2)}) copy-start(f32[8]{0:T(128)} %param.18) | copy-start | bytes 100
  2.0 0.7 %copy-start.8 = (f32[8]{0:T(128)S(1)}, f32[8]{0:T(128)}, u32[]{:S(2)}) copy-start(f32[8]{0:T(128)} %param.19) | copy-start | bytes 100
  2.0 0.7 %copy-start.9 = (s32[128]{0:T(128)S(1)}, s32[128]{0:T(128)}, u32[]{:S(2)}) copy-start(s32[128]{0:T(128)} %param.22) | copy-start | bytes 1540
  2.0 0.7 %copy-start.10 = (s32[128]{0:T(128)S(1)}, s32[128]{0:T(128)}, u32[]{:S(2)}) copy-start(s32[128]{0:T(128)} %param.23) | copy-start | bytes 1540
  2.0 0.7 %copy-start.11 = (s32[128]{0:T(128)S(1)}, s32[128]{0:T(128)}, u32[]{:S(2)}) copy-start(s32[128]{0:T(128)} %param.25) | copy-start | bytes 1540
  2.0 0.7 %copy-start.12 = (f32[128]{0:T(128)S(1)}, f32[128]{0:T(128)}, u32[]{:S(2)}) copy-start(f32[128]{0:T(128)} %param.26) | copy-start | bytes 1540
  2.8 1.2 %copy-start = (bf16[32,1,128,128]{3,2,1,0:T(8,128)(2,1)S(1)}, bf16[32,1,128,128]{3,2,1,0:T(8,128)(2,1)}, u32[]{:S(2)}) copy-start(bf16[32,1,128,128]{3,2,1,0:T(8,128)(2,1)} %param.20) | copy-start | bytes 3145732
  4.0 1.0 %copy-start.1 = (bf16[7,8,4096]{2,1,0:T(8,128)(2,1)S(1)}, bf16[7,8,4096]{2,1,0:T(8,128)(2,1)}, u32[]{:S(2)}) copy-start(bf16[7,8,4096]{2,1,0:T(8,128)(2,1)} %hist_ref.1) | copy-start | bytes 1376260
  5.0 0.9 %copy-start.2 = (f32[8,4096]{1,0:T(8,128)S(1)}, f32[8,4096]{1,0:T(8,128)}, u32[]{:S(2)}) copy-start(f32[8,4096]{1,0:T(8,128)} %act_ref.1) | copy-start | bytes 393220

commit v2 on v1

--- a/solution.py
+++ b/solution.py
@@ -10,7 +10,7 @@
 BLOCK = 128
 STEPS = 4
 HIST = 7
-CHUNKS = 4
+CHUNKS = 8
 MESH = pl.DeviceIdType.MESH
 
 
@@ -117,8 +117,8 @@
 def window(
     patches,
     groups,
-    act_ref,
-    hist_ref,
+    act_hbm,
+    hist_hbm,
     drive_ref,
     slope_ref,
     strength_ref,
@@ -135,6 +135,8 @@
     act_out,
     vaso_out,
     flow_out,
+    act_ref,
+    hist_ref,
     ht,
     hist2,
     send,
@@ -145,7 +147,11 @@
     meta_send,
     meta_recv,
     tiles,
-    ext,
+    ext0,
+    ext1,
+    ext2,
+    ext3,
+    ext4,
     halo_send,
     halo,
     coupling,
@@ -169,6 +175,7 @@
     vrecv_sem,
     local_sem,
 ):
+    ext = (ext0, ext1, ext2, ext3, ext4)
     f32, bf16, i32 = jnp.float32, jnp.bfloat16, jnp.int32
     n = patches
     nblk = 32
@@ -198,7 +205,11 @@
     def part(c):
         return pl.ds(c * (nblk // CHUNKS), nblk // CHUNKS)
 
-    own_tiles = pltpu.make_async_copy(kern_ref, tiles.at[grp], local_sem)
+    own_history = pltpu.make_async_copy(hist_hbm, hist_ref, local_sem.at[1])
+    own_history.start()
+    own_activity = pltpu.make_async_copy(act_hbm, act_ref, local_sem.at[2])
+    own_activity.start()
+    own_tiles = pltpu.make_async_copy(kern_ref, tiles.at[grp], local_sem.at[0])
     own_tiles.start()
 
     def tile_far(k, c):
@@ -260,8 +271,8 @@
     has_left, has_right = me > 0, me < n - 1
 
     def halo_start(s):
-        halo_send[s, 0] = ext[s, nblk]
-        halo_send[s, 1] = ext[s, 1]
+        halo_send[s, 0] = ext[s][nblk]
+        halo_send[s, 1] = ext[s][1]
 
         @pl.when(has_right)
         def _():
@@ -275,22 +286,19 @@
         @pl.when(has_left)
         def _():
             halo_copy(s, 0).wait_recv()
-            ext[s, 0] = halo[s, 0]
+            ext[s][0] = halo[s, 0]
 
         @pl.when(has_right)
         def _():
             halo_copy(s, 1).wait_recv()
-            ext[s, nblk + 1] = halo[s, 1]
+            ext[s][nblk + 1] = halo[s, 1]
 
     sub = lax.broadcasted_iota(i32, (128, 128), 0)
     lane = lax.broadcasted_iota(i32, (128, 128), 1)
     eye = sub == lane
 
-    def row_of(col):
-        return jnp.sum(jnp.where(eye, col, 0.0), axis=0, keepdims=True)
-
-    target_col = jnp.broadcast_to(target_ref[...].astype(f32), (128, 128))
-    target_row = row_of(target_col)
+    target_row = target_ref[...].astype(f32)
+    target_col = jnp.sum(jnp.where(eye, target_row, 0.0), axis=1, keepdims=True)
     same = target_col == target_row
     rank_row = jnp.sum(jnp.where(same & (sub < lane), 1.0, 0.0), axis=0, keepdims=True)
     rank_col = jnp.sum(jnp.where(same & (lane < sub), 1.0, 0.0), axis=1, keepdims=True)
@@ -318,6 +326,7 @@
             hist2[rows, j * 128 : (j + 1) * 128] = ht[lag, j * nblk : (j + 1) * nblk, :].astype(bf16)
         return 0
 
+    own_history.wait()
     lax.fori_loop(0, HIST, turn, 0)
     hist2[HIST * nblk :, :] = jnp.zeros((nblk, 1024), bf16)
 
@@ -342,11 +351,12 @@
     for q in range(n):
         meta_send[q] = jnp.broadcast_to(m[q : q + 1], (8, 256))
 
+    own_activity.wait()
     for b in range(nblk):
-        ext[0, b + 1] = act_ref[:, b * 128 : (b + 1) * 128]
+        ext[0][b + 1] = act_ref[:, b * 128 : (b + 1) * 128]
     for s in range(STEPS):
-        ext[s, 0] = jnp.zeros((8, 128), f32)
-        ext[s, nblk + 1] = jnp.zeros((8, 128), f32)
+        ext[s][0] = jnp.zeros((8, 128), f32)
+        ext[s][nblk + 1] = jnp.zeros((8, 128), f32)
 
     pl.semaphore_wait(barrier, n + 1)
     for c in range(CHUNKS):
@@ -425,19 +435,22 @@
         for j in range(8):
             coupling[s, j * nblk : (j + 1) * nblk, :] = total[:, j * 128 : (j + 1) * 128]
 
-    def update(s, b):
-        lhs = jnp.concatenate([ext[s, index_ref[b, k]] for k in range(4)], axis=1).astype(bf16)
-        rhs = jnp.concatenate([tiles[k, b] for k in range(4)], axis=0)
-        local = jnp.dot(lhs, rhs, preferred_element_type=f32)
-        tract = coupling[s, pl.ds(b, 8, stride=nblk), :]
-        pre = slope * (local + strength * tract + drive_ref[pl.ds(b, 1), :])
-        rate = ext[s, b + 1]
-        ext[s + 1, b + 1] = rate + 0.5 * (jax.nn.sigmoid(pre) - rate)
+    def update(s, blocks):
+        rates = []
+        for b in blocks:
+            lhs = jnp.concatenate([ext[s][index_ref[k, b]] for k in range(4)], axis=1).astype(bf16)
+            rhs = jnp.concatenate([tiles[k, b] for k in range(4)], axis=0)
+            local = jnp.dot(lhs, rhs, preferred_element_type=f32)
+            tract = coupling[s, pl.ds(b, 8, stride=nblk), :]
+            pre = slope * (local + strength * tract + drive_ref[pl.ds(b, 1), :])
+            rate = ext[s][b + 1]
+            rates.append(rate + 0.5 * (jax.nn.sigmoid(pre) - rate))
+        for b, rate in zip(blocks, rates):
+            ext[s + 1][b + 1] = rate
 
     def updates(s, low, high, width):
         def some(i, _):
-            for u in range(width):
-                update(s, low + i * width + u)
+            update(s, [low + i * width + u for u in range(width)])
             return 0
 
         lax.fori_loop(0, (high - low) // width, some, 0)
@@ -459,18 +472,17 @@
 
     for s in range(1, STEPS):
         couple(s)
-        updates(s, 1, nblk - 1, 10)
+        updates(s, 1, nblk - 1, 15)
         halo_take(s)
-        update(s, 0)
-        update(s, nblk - 1)
+        update(s, [0, nblk - 1])
         if s + 1 < STEPS:
             halo_start(s + 1)
 
-    ones = jnp.ones((16, 512), bf16)
+    ones = jnp.ones((64, 512), bf16)
 
     def sums(i, total):
         rates = [
-            jnp.concatenate([ext[s + 1, i * 4 + u + 1] for u in range(4)], axis=1)
+            jnp.concatenate([ext[s + 1][i * 4 + u + 1] for u in range(4)], axis=1)
             for s in range(STEPS)
         ]
         rates = jnp.concatenate(rates, axis=0)
@@ -479,10 +491,11 @@
         lhs = jnp.concatenate([high, low, ones], axis=0)
         rhs = jnp.concatenate([owned[i * 4 + u] for u in range(4)], axis=1)
         return total + lax.dot_general(
-            lhs, rhs, (((1,), (1,)), ((), ())), preferred_element_type=f32
-        )
-
-    total = lax.fori_loop(0, nblk // 4, sums, jnp.zeros((80, 384), f32))
+            rhs, lhs, (((1,), (1,)), ((), ())), preferred_element_type=f32
+        )
+
+    total = lax.fori_loop(0, nblk // 4, sums, jnp.zeros((384, 128), f32))
+    total = total.T
     total = jnp.concatenate([total[0:32] + total[32:64], total[64:72]], axis=0)
     vox_send[0] = total[:, 256:384]
     vox_send[1] = total[:, 0:128]
@@ -497,7 +510,7 @@
 
     vox_send[2] = total[:, 128:256]
     for b in range(nblk):
-        act_out[:, b * 128 : (b + 1) * 128] = ext[STEPS, b + 1]
+        act_out[:, b * 128 : (b + 1) * 128] = ext[STEPS][b + 1]
 
     @pl.when(has_left)
     def _():
@@ -565,7 +578,10 @@
     vmem = pl.BlockSpec(memory_space=pltpu.VMEM)
     smem = pl.BlockSpec(memory_space=pltpu.SMEM)
     dma = pltpu.SemaphoreType.DMA
+    hbm = pl.BlockSpec(memory_space=pltpu.HBM)
     scratch = [
+        pltpu.VMEM(activity.shape, f32),
+        pltpu.VMEM(history.shape, bf16),
         pltpu.VMEM((HIST, 256, 128), f32),
         pltpu.VMEM((256, 1024), bf16),
         pltpu.VMEM((STEPS, 128, 1024), bf16),
@@ -576,7 +592,7 @@
         pltpu.VMEM((n, 8, 256), f32),
         pltpu.VMEM((n, 8, 256), f32),
         pltpu.VMEM((4, 32, 128, 128), bf16),
-        pltpu.VMEM((STEPS + 1, 34, 8, 128), f32),
+        *[pltpu.VMEM((34, 8, 128), f32) for _ in range(STEPS + 1)],
         pltpu.VMEM((STEPS, 2, 8, 128), f32),
         pltpu.VMEM((STEPS, 2, 8, 128), f32),
         pltpu.VMEM((STEPS, 256, 128), f32),
@@ -598,7 +614,7 @@
         dma((STEPS, 2)),
         dma((2,)),
         dma((2,)),
-        dma,
+        dma((3,)),
     ]
     return pl.pallas_call(
         functools.partial(window, n, groups),
@@ -607,11 +623,11 @@
             jax.ShapeDtypeStruct(vaso_signal.shape, f32),
             jax.ShapeDtypeStruct(blood_flow.shape, f32),
         ),
-        in_specs=[vmem] * 6 + [smem] + [vmem] * 8,
+        in_specs=[hbm] * 2 + [vmem] * 3 + [hbm, smem] + [vmem] * 8,
         out_specs=(vmem, vmem, vmem),
         scratch_shapes=scratch,
         compiler_params=pltpu.CompilerParams(
-            collective_id=0, has_side_effects=True, vmem_limit_bytes=40 * 1024 * 1024
+            collective_id=0, has_side_effects=True, vmem_limit_bytes=62 * 1024 * 1024
         ),
     )(
         activity,
@@ -620,10 +636,10 @@
         slope.reshape(1, 8),
         strength.reshape(1, 8),
         kernel.reshape(32, 128, 128),
-        kernel_index,
+        kernel_index.T,
         tract_source.reshape(1, 128),
         tract_delay.reshape(1, 128),
-        tract_target,
+        tract_target.reshape(1, 128),
         tract_block.reshape(1, 128),
         tract_weight.reshape(1, 128),
         voxel_owner.reshape(32, 128),

time: 61.8 us -> 54.7 us (0.89)
  local copies, waits for them, and re-layouts: 7.05 us -> 2.84 us
  Pallas kernels: 53.7 us -> 51 us
    unnamed x35 -> x7, local copies, waits for them, and re-layouts: 7.05 us -> 2.84 us
    pallas_call x1, Pallas kernels: 53.7 us -> 51 us  [fused(): pl.pallas_call(functools.partial(window, n, groups), out_shape=(jax.Shape...]
where the time goes in v2:
time: 54.7 us; the launch traced here: 54.5 us
  Pallas kernels  51 us (93%)
  local copies, waits for them, and re-layouts  2.84 us (5%)
  between operations  0.66 us (1%)
    pallas_call x1, Pallas kernels, fused(): pl.pallas_call(functools.partial(window, n, groups), out_shape=(jax.Shape...  51 us
    unnamed x7, local copies, waits for them, and re-layouts  2.84 us

profile of v2, /device:TPU:0, one launch (start us, length us, event | category | flops | bytes accessed | tf_op | source)
XLA Modules:
  0.0 54.5 jit_solution(5521876763727210181)
XLA Ops:
  0.6 51.0 %shard_map.166 = (f32[8,4096]{1,0:T(8,128)}, f32[8,128]{1,0:T(8,128)}, f32[8,128]{1,0:T(8,128)}) custom-call(f32[8,4096]{1,0:T(8,128)} %act_hbm.1, bf16[7,8,4096]{2,1,0:T(8,128)(2,1)} %hist_hbm.1, f32[32,128]{1,0:T(8,128)} %bitcast.12, f32[1,8]{1,0:T(1,128)} %bitcast.15, f32[1,8]{1,0:T(1,128)} %bitcast.16, bf16[32,128,128]{2,1,0:T(8,128)(2,1)} %bitcast.11, ...), custom_call_target="tpu_custom_call" | custom-call | tf_op jit(solution)/shard_map/pallas_call | solution.py:619
  51.6 0.0 copy-start.1
  51.6 1.6 %copy.21 = f32[8,4096]{1,0:T(8,128)} copy(f32[8,4096]{1,0:T(8,128)} %get-tuple-element.6) | data formatting | bytes 262144
  53.2 0.0 copy-done.1
  53.2 0.0 copy-start
  53.2 0.6 %copy.22 = f32[8,128]{1,0:T(8,128)} copy(f32[8,128]{1,0:T(8,128)S(1)} %copy-done.1) | data formatting | bytes 8192
  53.8 0.1 copy-done
  53.9 0.6 %copy.23 = f32[8,128]{1,0:T(8,128)} copy(f32[8,128]{1,0:T(8,128)S(1)} %copy-done) | data formatting | bytes 8192
Async XLA Ops:
  51.6 1.6 %copy-start.1 = (f32[8,128]{1,0:T(8,128)S(1)}, f32[8,128]{1,0:T(8,128)}, u32[]{:S(2)}) copy-start(f32[8,128]{1,0:T(8,128)} %get-tuple-element.7) | copy-start | bytes 12292
  53.2 0.7 %copy-start = (f32[8,128]{1,0:T(8,128)S(1)}, f32[8,128]{1,0:T(8,128)}, u32[]{:S(2)}) copy-start(f32[8,128]{1,0:T(8,128)} %get-tuple-element.8) | copy-start | bytes 12292

commit v3 on v2

--- a/solution.py
+++ b/solution.py
@@ -10,7 +10,7 @@
 BLOCK = 128
 STEPS = 4
 HIST = 7
-CHUNKS = 8
+STAGES = 4
 MESH = pl.DeviceIdType.MESH
 
 
@@ -202,8 +202,11 @@
             device_id_type=MESH,
         )
 
-    def part(c):
-        return pl.ds(c * (nblk // CHUNKS), nblk // CHUNKS)
+    wide_part = nblk // (2 * STAGES)
+
+    def part(m, side):
+        low = m * wide_part if side == 0 else nblk - (m + 1) * wide_part
+        return pl.ds(low, wide_part)
 
     own_history = pltpu.make_async_copy(hist_hbm, hist_ref, local_sem.at[1])
     own_history.start()
@@ -212,24 +215,24 @@
     own_tiles = pltpu.make_async_copy(kern_ref, tiles.at[grp], local_sem.at[0])
     own_tiles.start()
 
-    def tile_far(k, c):
+    def tile_far(k, m, side):
         return remote(
-            kern_ref.at[part(c)],
-            tiles.at[k, part(c)],
-            xsend_sem.at[c],
-            xrecv_sem.at[c],
+            kern_ref.at[part(m, side)],
+            tiles.at[k, part(m, side)],
+            xsend_sem.at[m, side],
+            xrecv_sem.at[m, side],
             {"trial": far},
         )
 
     def tile_near(k):
         return remote(kern_ref, tiles.at[k], csem.at[0], csem.at[1], {"trial": near})
 
-    def tile_relay(k, c):
+    def tile_relay(k, m, side):
         return remote(
-            tiles.at[k, part(c)],
-            tiles.at[k, part(c)],
-            rsend_sem.at[c],
-            rrecv_sem.at[c],
+            tiles.at[k, part(m, side)],
+            tiles.at[k, part(m, side)],
+            rsend_sem.at[m, side],
+            rrecv_sem.at[m, side],
             {"trial": near},
         )
 
@@ -359,33 +362,38 @@
         ext[s][nblk + 1] = jnp.zeros((8, 128), f32)
 
     pl.semaphore_wait(barrier, n + 1)
-    for c in range(CHUNKS):
-        tile_far(grp, c).start()
-    for d in range(1, n):
-        main_copy(0, me, lax.rem(me + d, n)).start()
+    def tiles_start(m):
+        for side in range(2):
+            tile_far(grp, m, side).start()
+
+    def tracts_start(s):
+        for d in range(1, n):
+            main_copy(s, me, lax.rem(me + d, n)).start()
+
+    tracts_start(0)
+    tiles_start(0)
     tile_near(grp).start()
     halo_start(0)
     for d in range(1, n):
         meta_copy(me, lax.rem(me + d, n)).start()
-    for s in range(1, STEPS):
+    choose = jnp.concatenate(
+        [jnp.where(wide8 == key_over - float(t * nblk), 1.0, 0.0) for t in range(STEPS)], axis=0
+    ).astype(bf16)
+    rows = jnp.dot(choose, hist2[...], preferred_element_type=f32)
+    for t in range(STEPS):
+        for j in range(8):
+            over_f[pl.ds(t * 8 + j, n, stride=32), :] = (
+                rows[t * 8 : t * 8 + 8, j * 128 : (j + 1) * 128] * weight_over
+            )
+    for q in range(n):
+        over_send[q] = over_f[q * 32 : (q + 1) * 32, :].astype(bf16)
+    for d in range(1, n):
+        over_copy(me, lax.rem(me + d, n)).start()
+    gathered(1)
+    tracts_start(1)
+    tiles_start(1)
+    for s in range(2, STEPS):
         gathered(s)
-        for d in range(1, n):
-            main_copy(s, me, lax.rem(me + d, n)).start()
-        if s == 1:
-            choose = jnp.concatenate(
-                [jnp.where(wide8 == key_over - float(t * nblk), 1.0, 0.0) for t in range(STEPS)],
-                axis=0,
-            ).astype(bf16)
-            rows = jnp.dot(choose, hist2[...], preferred_element_type=f32)
-            for t in range(STEPS):
-                for j in range(8):
-                    over_f[pl.ds(t * 8 + j, n, stride=32), :] = (
-                        rows[t * 8 : t * 8 + 8, j * 128 : (j + 1) * 128] * weight_over
-                    )
-            for q in range(n):
-                over_send[q] = over_f[q * 32 : (q + 1) * 32, :].astype(bf16)
-            for d in range(1, n):
-                over_copy(me, lax.rem(me + d, n)).start()
 
     mine16 = pl.ds(pl.multiple_of(me * 16, 16), 16)
     for s in range(STEPS):
@@ -394,7 +402,9 @@
     meta_recv[me] = meta_send[me]
 
     first = ((me - 1) * 128).astype(f32)
-    vox_id = lax.broadcasted_iota(i32, (384, 128), 0).astype(f32) + first
+    row_id = lax.broadcasted_iota(i32, (288, 128), 0)
+    vox_id = (row_id + jnp.where(row_id >= 96, 32, 0) + jnp.where(row_id >= 192, 32, 0)).astype(f32)
+    vox_id = vox_id + first
 
     def member(b, _):
         owner = owner_ref[pl.ds(b, 1), :].astype(f32)
@@ -448,35 +458,43 @@
         for b, rate in zip(blocks, rates):
             ext[s + 1][b + 1] = rate
 
-    def updates(s, low, high, width):
-        def some(i, _):
-            update(s, [low + i * width + u for u in range(width)])
-            return 0
-
-        lax.fori_loop(0, (high - low) // width, some, 0)
-
-    couple(0)
-    halo_take(0)
+    def region(s, m):
+        if s > m:
+            return set()
+        reach = (m + 1) * wide_part - s
+        if m == STAGES - 1:
+            reach = nblk // 2
+        return set(range(reach)) | set(range(nblk - reach, nblk))
+
+    def step(s, m):
+        todo = sorted(region(s, m) - (region(s, m - 1) if m > 0 else set()))
+        for i in range(0, len(todo), 16):
+            update(s, todo[i : i + 16])
+
     own_tiles.wait()
     tile_near(near).wait_recv()
-    tile_far(far, 0).wait_recv()
-    tile_relay(far, 0).start()
     other = lax.rem(near + 2, groups)
-    for c in range(CHUNKS):
-        if c + 1 < CHUNKS:
-            tile_far(far, c + 1).wait_recv()
-            tile_relay(far, c + 1).start()
-        tile_relay(other, c).wait_recv()
-        updates(0, c * (nblk // CHUNKS), (c + 1) * (nblk // CHUNKS), nblk // CHUNKS)
-    halo_start(1)
-
-    for s in range(1, STEPS):
-        couple(s)
-        updates(s, 1, nblk - 1, 15)
-        halo_take(s)
-        update(s, [0, nblk - 1])
-        if s + 1 < STEPS:
-            halo_start(s + 1)
+    for m in range(STAGES):
+        for side in range(2):
+            tile_far(grp, m, side).wait_send()
+        if m + 2 < STAGES:
+            tiles_start(m + 2)
+        for d in range(1, n):
+            main_copy(m, me, lax.rem(me + d, n)).wait_send()
+        if m + 2 < STEPS:
+            tracts_start(m + 2)
+        for side in range(2):
+            tile_far(far, m, side).wait_recv()
+            tile_relay(far, m, side).start()
+        couple(m)
+        for side in range(2):
+            tile_relay(other, m, side).wait_recv()
+        for s in range(m + 1):
+            if s == m:
+                halo_take(s)
+            step(s, m)
+            if s == m and s + 1 < STEPS:
+                halo_start(s + 1)
 
     ones = jnp.ones((64, 512), bf16)
 
@@ -494,11 +512,14 @@
             rhs, lhs, (((1,), (1,)), ((), ())), preferred_element_type=f32
         )
 
-    total = lax.fori_loop(0, nblk // 4, sums, jnp.zeros((384, 128), f32))
-    total = total.T
-    total = jnp.concatenate([total[0:32] + total[32:64], total[64:72]], axis=0)
-    vox_send[0] = total[:, 256:384]
-    vox_send[1] = total[:, 0:128]
+    total = lax.fori_loop(0, nblk // 4, sums, jnp.zeros((288, 128), f32))
+
+    def of_patch(i):
+        rows = jnp.concatenate([total[i * 96 : (i + 1) * 96], jnp.zeros((32, 128), f32)], axis=0).T
+        return jnp.concatenate([rows[0:32] + rows[32:64], rows[64:72]], axis=0)
+
+    vox_send[0] = of_patch(2)
+    vox_send[1] = of_patch(0)
 
     @pl.when(has_right)
     def _():
@@ -508,7 +529,7 @@
     def _():
         vox_copy(1).start()
 
-    vox_send[2] = total[:, 128:256]
+    vox_send[2] = of_patch(1)
     for b in range(nblk):
         act_out[:, b * 128 : (b + 1) * 128] = ext[STEPS][b + 1]
 
@@ -534,14 +555,12 @@
 
     for d in range(1, n):
         q = lax.rem(me + d, n)
-        for s in range(STEPS):
-            main_copy(s, me, q).wait_send()
         over_copy(me, q).wait_send()
         meta_copy(me, q).wait_send()
     tile_near(grp).wait_send()
-    for c in range(CHUNKS):
-        tile_far(grp, c).wait_send()
-        tile_relay(far, c).wait_send()
+    for m in range(STAGES):
+        for side in range(2):
+            tile_relay(far, m, side).wait_send()
 
     @pl.when(has_right)
     def _():
@@ -554,6 +573,17 @@
         for s in range(STEPS):
             halo_copy(s, 1).wait_send()
         vox_copy(1).wait_send()
+
+
+def hand_on(a, b, c, a_out, b_out, c_out, sems):
+    copies = [
+        pltpu.make_async_copy(src, dst, sems.at[i])
+        for i, (src, dst) in enumerate(((a, a_out), (b, b_out), (c, c_out)))
+    ]
+    for copy in copies:
+        copy.start()
+    for copy in copies:
+        copy.wait()
 
 
 def fused(
@@ -596,7 +626,7 @@
         pltpu.VMEM((STEPS, 2, 8, 128), f32),
         pltpu.VMEM((STEPS, 2, 8, 128), f32),
         pltpu.VMEM((STEPS, 256, 128), f32),
-        pltpu.VMEM((32, 384, 128), bf16),
+        pltpu.VMEM((32, 288, 128), bf16),
         pltpu.VMEM((3, 40, 128), f32),
         pltpu.VMEM((2, 40, 128), f32),
         dma((STEPS, n)),
@@ -605,10 +635,10 @@
         dma((n,)),
         dma((n,)),
         dma((n,)),
-        dma((CHUNKS,)),
-        dma((CHUNKS,)),
-        dma((CHUNKS,)),
-        dma((CHUNKS,)),
+        dma((STAGES, 2)),
+        dma((STAGES, 2)),
+        dma((STAGES, 2)),
+        dma((STAGES, 2)),
         dma((2,)),
         dma((STEPS, 2)),
         dma((STEPS, 2)),
@@ -616,7 +646,7 @@
         dma((2,)),
         dma((3,)),
     ]
-    return pl.pallas_call(
+    results = pl.pallas_call(
         functools.partial(window, n, groups),
         out_shape=(
             jax.ShapeDtypeStruct(activity.shape, f32),
@@ -646,6 +676,14 @@
         vaso_signal,
         blood_flow,
     )
+    return pl.pallas_call(
+        hand_on,
+        out_shape=tuple(jax.ShapeDtypeStruct(r.shape, r.dtype) for r in results),
+        in_specs=[hbm] * 3,
+        out_specs=(hbm, hbm, hbm),
+        scratch_shapes=[dma((3,))],
+        compiler_params=pltpu.CompilerParams(vmem_limit_bytes=62 * 1024 * 1024),
+    )(*results)
 
 
 def planned(*args):

time: 54.7 us -> 51.7 us (0.945)
  local copies, waits for them, and re-layouts: 2.84 us -> 0 us
    pallas_call x1, Pallas kernels: 51 us -> 45.5 us  [fused(): pl.pallas_call(functools.partial(window, n, groups), out_shape=(jax.Shape...]
    pallas_call x0 -> x1, Pallas kernels: none -> 5.35 us  [fused(): pl.pallas_call(hand_on, out_shape=tuple((jax.ShapeDtypeStruct(r.shape, r....]
    unnamed x7 -> x0, local copies, waits for them, and re-layouts: 2.84 us -> none
where the time goes in v3:
time: 51.7 us; the launch traced here: 51.5 us
  Pallas kernels  50.8 us (98%)
  between operations  0.64 us (1%)
    pallas_call x1, Pallas kernels, fused(): pl.pallas_call(functools.partial(window, n, groups), out_shape=(jax.Shape...  45.5 us
    pallas_call x1, Pallas kernels, fused(): pl.pallas_call(hand_on, out_shape=tuple((jax.ShapeDtypeStruct(r.shape, r....  5.35 us

profile of v3, /device:TPU:0, one launch (start us, length us, event | category | flops | bytes accessed | tf_op | source)
XLA Modules:
  0.0 51.5 jit_solution(16954192896220859422)
XLA Ops:
  0.6 45.5 %shard_map.166 = (f32[8,4096]{1,0:T(8,128)}, f32[8,128]{1,0:T(8,128)}, f32[8,128]{1,0:T(8,128)}) custom-call(f32[8,4096]{1,0:T(8,128)} %act_hbm.1, bf16[7,8,4096]{2,1,0:T(8,128)(2,1)} %hist_hbm.1, f32[32,128]{1,0:T(8,128)} %bitcast.12, f32[1,8]{1,0:T(1,128)} %bitcast.15, f32[1,8]{1,0:T(1,128)} %bitcast.16, bf16[32,128,128]{2,1,0:T(8,128)(2,1)} %bitcast.11, ...), custom_call_target="tpu_custom_call" | custom-call | tf_op jit(solution)/shard_map/pallas_call | solution.py:649
  46.1 5.3 %shard_map.167 = (f32[8,4096]{1,0:T(8,128)}, f32[8,128]{1,0:T(8,128)}, f32[8,128]{1,0:T(8,128)}) custom-call(f32[8,4096]{1,0:T(8,128)} %get-tuple-element.6.a, f32[8,128]{1,0:T(8,128)} %get-tuple-element.7.b, f32[8,128]{1,0:T(8,128)} %get-tuple-element.8.c), custom_call_target="tpu_custom_call" | custom-call | tf_op jit(solution)/shard_map/pallas_call | solution.py:679

commit v4 on v3

--- a/solution.py
+++ b/solution.py
@@ -299,13 +299,14 @@
     sub = lax.broadcasted_iota(i32, (128, 128), 0)
     lane = lax.broadcasted_iota(i32, (128, 128), 1)
     eye = sub == lane
+    lanes = lane.astype(f32)
 
     target_row = target_ref[...].astype(f32)
     target_col = jnp.sum(jnp.where(eye, target_row, 0.0), axis=1, keepdims=True)
     same = target_col == target_row
     rank_row = jnp.sum(jnp.where(same & (sub < lane), 1.0, 0.0), axis=0, keepdims=True)
     rank_col = jnp.sum(jnp.where(same & (lane < sub), 1.0, 0.0), axis=1, keepdims=True)
-    key_row = ((delay_ref[...] - 1) * nblk + source_ref[...]).astype(f32)
+    key_row = ((delay_ref[...] - STEPS) * nblk + source_ref[...]).astype(f32)
     weight_row = weight_ref[...]
     slot_row = jnp.where(rank_row < 16.0, target_row * 16.0 + rank_row, -1.0)
     sel = sub.astype(f32) == slot_row
@@ -329,22 +330,31 @@
             hist2[rows, j * 128 : (j + 1) * 128] = ht[lag, j * nblk : (j + 1) * nblk, :].astype(bf16)
         return 0
 
+    def tiles_start(m):
+        for side in range(2):
+            tile_far(grp, m, side).start()
+
+    def tracts_start(s):
+        for d in range(1, n):
+            main_copy(s, me, lax.rem(me + d, n)).start()
+
+    pl.semaphore_wait(barrier, n + 1)
+    tiles_start(0)
+    tile_near(grp).start()
+
+    choose = jnp.where(lanes == key, 1.0, 0.0).astype(bf16)
+
+    def gathered(s):
+        low = (STEPS - 1 - s) * nblk
+        rows = jnp.dot(choose, hist2[low : low + 128, :], preferred_element_type=f32)
+        send[s] = (rows * weight).astype(bf16)
+
     own_history.wait()
-    lax.fori_loop(0, HIST, turn, 0)
-    hist2[HIST * nblk :, :] = jnp.zeros((nblk, 1024), bf16)
-
-    wide = lax.broadcasted_iota(i32, (128, 256), 1).astype(f32)
-    wide8 = lax.broadcasted_iota(i32, (n, 256), 1).astype(f32)
-
-    def gathered(s):
-        choose = jnp.where(wide == key - float(s * nblk), 1.0, 0.0).astype(bf16)
-        rows = jnp.dot(choose, hist2[...], preferred_element_type=f32)
-        send[s] = (rows * weight).astype(bf16)
-
+    lax.fori_loop(STEPS - 1, HIST, turn, 0)
     gathered(0)
+    tracts_start(0)
 
     a = jnp.where(q8 == target_row, block_ref[...].astype(f32), 0.0).astype(bf16)
-    lanes = lane.astype(f32)
     mef = me.astype(f32)
     b1 = jnp.where((rank_col < 16.0) & (lanes == rank_col + mef * 16.0), 1.0, 0.0).astype(bf16)
     b2 = jnp.where((rank_col == 16.0) & (lanes == mef), 1.0, 0.0).astype(bf16)
@@ -361,37 +371,25 @@
         ext[s][0] = jnp.zeros((8, 128), f32)
         ext[s][nblk + 1] = jnp.zeros((8, 128), f32)
 
-    pl.semaphore_wait(barrier, n + 1)
-    def tiles_start(m):
-        for side in range(2):
-            tile_far(grp, m, side).start()
-
-    def tracts_start(s):
-        for d in range(1, n):
-            main_copy(s, me, lax.rem(me + d, n)).start()
-
-    tracts_start(0)
-    tiles_start(0)
-    tile_near(grp).start()
     halo_start(0)
     for d in range(1, n):
         meta_copy(me, lax.rem(me + d, n)).start()
-    choose = jnp.concatenate(
-        [jnp.where(wide8 == key_over - float(t * nblk), 1.0, 0.0) for t in range(STEPS)], axis=0
-    ).astype(bf16)
-    rows = jnp.dot(choose, hist2[...], preferred_element_type=f32)
+    lax.fori_loop(0, STEPS - 1, turn, 0)
+    gathered(1)
+    tracts_start(1)
+    tiles_start(1)
+    choose_over = jnp.where(lanes[0:n] == key_over, 1.0, 0.0).astype(bf16)
     for t in range(STEPS):
+        low = (STEPS - 1 - t) * nblk
+        rows = jnp.dot(choose_over, hist2[low : low + 128, :], preferred_element_type=f32)
         for j in range(8):
             over_f[pl.ds(t * 8 + j, n, stride=32), :] = (
-                rows[t * 8 : t * 8 + 8, j * 128 : (j + 1) * 128] * weight_over
+                rows[:, j * 128 : (j + 1) * 128] * weight_over
             )
     for q in range(n):
         over_send[q] = over_f[q * 32 : (q + 1) * 32, :].astype(bf16)
     for d in range(1, n):
         over_copy(me, lax.rem(me + d, n)).start()
-    gathered(1)
-    tracts_start(1)
-    tiles_start(1)
     for s in range(2, STEPS):
         gathered(s)
 
@@ -512,7 +510,9 @@
             rhs, lhs, (((1,), (1,)), ((), ())), preferred_element_type=f32
         )
 
-    total = lax.fori_loop(0, nblk // 4, sums, jnp.zeros((288, 128), f32))
+    total = jnp.zeros((288, 128), f32)
+    for i in range(nblk // 4):
+        total = sums(i, total)
 
     def of_patch(i):
         rows = jnp.concatenate([total[i * 96 : (i + 1) * 96], jnp.zeros((32, 128), f32)], axis=0).T
@@ -575,15 +575,10 @@
         vox_copy(1).wait_send()
 
 
-def hand_on(a, b, c, a_out, b_out, c_out, sems):
-    copies = [
-        pltpu.make_async_copy(src, dst, sems.at[i])
-        for i, (src, dst) in enumerate(((a, a_out), (b, b_out), (c, c_out)))
-    ]
-    for copy in copies:
-        copy.start()
-    for copy in copies:
-        copy.wait()
+def hand_on(a, b, c, a_out, b_out, c_out):
+    a_out[...] = a[...]
+    b_out[...] = b[...]
+    c_out[...] = c[...]
 
 
 def fused(
@@ -613,7 +608,7 @@
         pltpu.VMEM(activity.shape, f32),
         pltpu.VMEM(history.shape, bf16),
         pltpu.VMEM((HIST, 256, 128), f32),
-        pltpu.VMEM((256, 1024), bf16),
+        pltpu.VMEM((HIST * 32, 1024), bf16),
         pltpu.VMEM((STEPS, 128, 1024), bf16),
         pltpu.VMEM((STEPS, 144, 1024), bf16),
         pltpu.VMEM((256, 128), f32),
@@ -679,9 +674,8 @@
     return pl.pallas_call(
         hand_on,
         out_shape=tuple(jax.ShapeDtypeStruct(r.shape, r.dtype) for r in results),
-        in_specs=[hbm] * 3,
-        out_specs=(hbm, hbm, hbm),
-        scratch_shapes=[dma((3,))],
+        in_specs=[vmem] * 3,
+        out_specs=(vmem, vmem, vmem),
         compiler_params=pltpu.CompilerParams(vmem_limit_bytes=62 * 1024 * 1024),
     )(*results)
 

time: 51.7 us -> 48.3 us (0.934)
  Pallas kernels: 50.8 us -> 47.4 us
    pallas_call x1, Pallas kernels: 5.35 us -> 1.58 us  [fused(): pl.pallas_call(hand_on, out_shape=tuple((jax.ShapeDtypeStruct(r.shape, r....]
where the time goes in v4:
time: 48.3 us; the launch traced here: 48.1 us
  Pallas kernels  47.4 us (98%)
  between operations  0.64 us (1%)
    pallas_call x1, Pallas kernels, fused(): pl.pallas_call(functools.partial(window, n, groups), out_shape=(jax.Shape...  45.8 us
    pallas_call x1, Pallas kernels, fused(): pl.pallas_call(hand_on, out_shape=tuple((jax.ShapeDtypeStruct(r.shape, r....  1.58 us

profile of v4, /device:TPU:0, one launch (start us, length us, event | category | flops | bytes accessed | tf_op | source)
XLA Modules:
  0.0 48.1 jit_solution(11313977773218957335)
XLA Ops:
  0.6 45.8 %shard_map.166 = (f32[8,4096]{1,0:T(8,128)}, f32[8,128]{1,0:T(8,128)}, f32[8,128]{1,0:T(8,128)}) custom-call(f32[8,4096]{1,0:T(8,128)} %act_hbm.1, bf16[7,8,4096]{2,1,0:T(8,128)(2,1)} %hist_hbm.1, f32[32,128]{1,0:T(8,128)} %bitcast.12, f32[1,8]{1,0:T(1,128)} %bitcast.15, f32[1,8]{1,0:T(1,128)} %bitcast.16, bf16[32,128,128]{2,1,0:T(8,128)(2,1)} %bitcast.11, ...), custom_call_target="tpu_custom_call" | custom-call | tf_op jit(solution)/shard_map/pallas_call | solution.py:644
  46.5 1.6 %shard_map.167 = (f32[8,4096]{1,0:T(8,128)}, f32[8,128]{1,0:T(8,128)}, f32[8,128]{1,0:T(8,128)}) custom-call(f32[8,4096]{1,0:T(8,128)} %get-tuple-element.6.a, f32[8,128]{1,0:T(8,128)} %get-tuple-element.7.b, f32[8,128]{1,0:T(8,128)} %get-tuple-element.8.c), custom_call_target="tpu_custom_call" | custom-call | tf_op jit(solution)/shard_map/pallas_call | solution.py:674

commit v5 on v4

--- a/solution.py
+++ b/solution.py
@@ -339,7 +339,8 @@
             main_copy(s, me, lax.rem(me + d, n)).start()
 
     pl.semaphore_wait(barrier, n + 1)
-    tiles_start(0)
+    for m in range(STAGES):
+        tiles_start(m)
     tile_near(grp).start()
 
     choose = jnp.where(lanes == key, 1.0, 0.0).astype(bf16)
@@ -377,7 +378,6 @@
     lax.fori_loop(0, STEPS - 1, turn, 0)
     gathered(1)
     tracts_start(1)
-    tiles_start(1)
     choose_over = jnp.where(lanes[0:n] == key_over, 1.0, 0.0).astype(bf16)
     for t in range(STEPS):
         low = (STEPS - 1 - t) * nblk
@@ -392,6 +392,7 @@
         over_copy(me, lax.rem(me + d, n)).start()
     for s in range(2, STEPS):
         gathered(s)
+        tracts_start(s)
 
     mine16 = pl.ds(pl.multiple_of(me * 16, 16), 16)
     for s in range(STEPS):
@@ -475,12 +476,8 @@
     for m in range(STAGES):
         for side in range(2):
             tile_far(grp, m, side).wait_send()
-        if m + 2 < STAGES:
-            tiles_start(m + 2)
         for d in range(1, n):
             main_copy(m, me, lax.rem(me + d, n)).wait_send()
-        if m + 2 < STEPS:
-            tracts_start(m + 2)
         for side in range(2):
             tile_far(far, m, side).wait_recv()
             tile_relay(far, m, side).start()

time: 48.3 us -> 49.1 us (1.017)
  Pallas kernels: 47.4 us -> 48.3 us
    pallas_call x1, Pallas kernels: 45.8 us -> 46.7 us  [fused(): pl.pallas_call(functools.partial(window, n, groups), out_shape=(jax.Shape...]
where the time goes in v5:
time: 49.1 us; the launch traced here: 48.9 us
  Pallas kernels  48.3 us (98%)
  between operations  0.64 us (1%)
    pallas_call x1, Pallas kernels, fused(): pl.pallas_call(functools.partial(window, n, groups), out_shape=(jax.Shape...  46.7 us
    pallas_call x1, Pallas kernels, fused(): pl.pallas_call(hand_on, out_shape=tuple((jax.ShapeDtypeStruct(r.shape, r....  1.58 us

profile of v5, /device:TPU:0, one launch (start us, length us, event | category | flops | bytes accessed | tf_op | source)
XLA Modules:
  0.0 48.9 jit_solution(14286287848424390311)
XLA Ops:
  0.6 46.7 %shard_map.166 = (f32[8,4096]{1,0:T(8,128)}, f32[8,128]{1,0:T(8,128)}, f32[8,128]{1,0:T(8,128)}) custom-call(f32[8,4096]{1,0:T(8,128)} %act_hbm.1, bf16[7,8,4096]{2,1,0:T(8,128)(2,1)} %hist_hbm.1, f32[32,128]{1,0:T(8,128)} %bitcast.12, f32[1,8]{1,0:T(1,128)} %bitcast.15, f32[1,8]{1,0:T(1,128)} %bitcast.16, bf16[32,128,128]{2,1,0:T(8,128)(2,1)} %bitcast.11, ...), custom_call_target="tpu_custom_call" | custom-call | tf_op jit(solution)/shard_map/pallas_call | solution.py:641
  47.4 1.6 %shard_map.167 = (f32[8,4096]{1,0:T(8,128)}, f32[8,128]{1,0:T(8,128)}, f32[8,128]{1,0:T(8,128)}) custom-call(f32[8,4096]{1,0:T(8,128)} %get-tuple-element.6.a, f32[8,128]{1,0:T(8,128)} %get-tuple-element.7.b, f32[8,128]{1,0:T(8,128)} %get-tuple-element.8.c), custom_call_target="tpu_custom_call" | custom-call | tf_op jit(solution)/shard_map/pallas_call | solution.py:671
